TPU v7x, 32 devices: a whole 2x2x4 slice. The times are simulated.
32 devices in a mesh: section: 4 (over y, x), dp: 8 (over z, core).
Axes of the slice: x: 2, y: 2, z: 4, core: 2. Of those that a mesh axis runs over, the one named last changes fastest.
Arguments:
- tokens: bfloat16 [4, 8, 196, 256], P('section', 'dp'), may hold values from -6 to 6
- routes: int32 [4, 8, 2, 8, 49, 4], P('section', 'dp'), may hold values from 0 to 48, all different within a row
- pos_weight: bfloat16 [2, 9, 256], replicated, may hold values from -2 to 2
- attn_gain: bfloat16 [2, 256], replicated, may hold values from 0.5 to 1.5
- attn_bias: bfloat16 [2, 256], replicated, may hold values from -3 to 3
- qkv_weight: bfloat16 [2, 256, 768], replicated, may hold values from -0.375 to 0.375
- lepe_weight: bfloat16 [2, 25, 256], replicated, may hold values from -1.25 to 1.25
- proj_weight: bfloat16 [2, 256, 256], replicated, may hold values from -0.375 to 0.375
- mlp_gain: bfloat16 [2, 256], replicated, may hold values from 0.5 to 1.5
- mlp_bias: bfloat16 [2, 256], replicated, may hold values from -3 to 3
- fc1_weight: bfloat16 [2, 256, 768], replicated, may hold values from -0.375 to 0.375
- fc2_weight: bfloat16 [2, 768, 256], replicated, may hold values from -0.21875 to 0.21875
- cotangent: bfloat16 [4, 8, 196, 256], P('section', 'dp'), may hold values from -6 to 6
Outputs:
- block_output: bfloat16 [4, 8, 196, 256], P('section', 'dp')
- input_grad: bfloat16 [4, 8, 196, 256], P('section', 'dp')
- pos_grad: float32 [2, 9, 256], replicated
- attn_gain_grad: float32 [2, 256], replicated
- attn_bias_grad: float32 [2, 256], replicated
- qkv_grad: float32 [2, 256, 768], replicated
- lepe_grad: float32 [2, 25, 256], replicated
- proj_grad: float32 [2, 256, 256], replicated
- mlp_gain_grad: float32 [2, 256], replicated
- mlp_bias_grad: float32 [2, 256], replicated
- fc1_grad: float32 [2, 256, 768], replicated
- fc2_grad: float32 [2, 768, 256], replicated
Inputs may be any that keep to these rules, and one draw needn't show every extreme that they name: `routes`: each row of 4 names different regions.
All inputs are finite; a program needn't handle non-finite values.
Results may differ from a plain program's by a relative error of at most 0.018.
Values may be sent and summed in bfloat16 or wider, within the bound.
A program may use at most 320 MiB of HBM per device.

v0:
```python
from functools import partial
import math

import jax
import jax.numpy as jnp
from jax import lax
from jax.sharding import PartitionSpec as P

HEADS = 8
SIDE = 14
REG_SIDE = 7
TOPK = 4
HEAD_DIM = 32
REGIONS = 49


EPS = 1e-06


def for_sending(array):
    return jax.tree.map(lambda a: a.astype(jnp.bfloat16) if a.dtype == jnp.float32 else a, array)


def shifted(block, axis, distance):
    devices = range(lax.axis_size(axis))
    route = [(i - distance, i) for i in devices if i - distance in devices]
    return lax.ppermute(block, axis, route)


def from_root(block, axis, source):
    block = jnp.where(lax.axis_index(axis) == source, block, jnp.zeros_like(block))
    return lax.psum(block, axis)


def depthwise(signal, kernel):
    images = signal.shape[0]
    channels = signal.shape[-1]
    extent = math.isqrt(kernel.shape[0])
    radius = extent // 2
    picture = signal.reshape(images, SIDE, SIDE, channels)
    padded = jnp.pad(picture, ((0, 0), (radius, radius), (radius, radius), (0, 0)))
    summed = jnp.zeros_like(picture)
    for row_tap in range(extent):
        for col_tap in range(extent):
            summed = (
                summed
                + padded[:, row_tap : row_tap + SIDE, col_tap : col_tap + SIDE, :]
                * kernel[row_tap * extent + col_tap]
            )
    return summed.reshape(images, SIDE * SIDE, channels)


def norm_rows(signal, gain, bias):
    average = jnp.mean(signal, axis=-1, keepdims=True)
    centered = signal - average
    variance = jnp.mean(centered * centered, axis=-1, keepdims=True)
    return centered * lax.rsqrt(variance + EPS) * gain + bias


def exact_gelu(values):
    return jax.nn.gelu(values, approximate=False)


def to_regions(signal):
    images = signal.shape[0]
    channels = signal.shape[-1]
    patch_side = SIDE // REG_SIDE
    grid = signal.reshape(images, REG_SIDE, patch_side, REG_SIDE, patch_side, channels)
    return grid.transpose(0, 1, 3, 2, 4, 5).reshape(
        images, REG_SIDE * REG_SIDE, patch_side * patch_side, channels
    )


def from_regions(signal):
    images = signal.shape[0]
    channels = signal.shape[-1]
    patch_side = SIDE // REG_SIDE
    grid = signal.reshape(images, REG_SIDE, REG_SIDE, patch_side, patch_side, channels)
    return grid.transpose(0, 1, 3, 2, 4, 5).reshape(images, SIDE * SIDE, channels)


def heads_of(signal):
    regional = to_regions(signal)
    images, region_count, inside, channels = regional.shape
    return regional.reshape(images, region_count, inside, HEADS, channels // HEADS).transpose(
        0, 3, 1, 2, 4
    )


def merge_heads(signal):
    images, head_count, region_count, inside, head_width = signal.shape
    return from_regions(
        signal.transpose(0, 2, 3, 1, 4).reshape(
            images, region_count, inside, head_count * head_width
        )
    )


def gather_regions(onehot, signal):
    grouped = heads_of(signal)
    images, head_count, region_count, inside, head_width = grouped.shape
    grouped = grouped.reshape(images, head_count, region_count, inside * head_width)
    picked = jnp.einsum(
        "ihrjs,ihsm->ihrjm", onehot, grouped, preferred_element_type=jnp.float32
    ).astype(jnp.bfloat16)
    return picked.reshape(images, head_count, region_count, TOPK * inside, head_width)


def scatter_regions(onehot, grad_picked):
    images, head_count, region_count, keys_all, head_width = grad_picked.shape
    inside = keys_all // TOPK
    grouped = grad_picked.reshape(images, head_count, region_count, TOPK, inside * head_width)
    summed = jnp.einsum("ihrjs,ihrjm->ihsm", onehot, grouped, preferred_element_type=jnp.float32)
    return merge_heads(summed.reshape(images, head_count, region_count, inside, head_width))


def attn_pieces(inputs, routed, pos_w, gain, bias, qkv_w, lepe_w):
    images = inputs.shape[0]
    features = inputs.shape[-1]
    base_in = inputs.astype(jnp.float32)
    mixed_in = base_in + depthwise(base_in, pos_w.astype(jnp.float32))
    normed = norm_rows(mixed_in, gain.astype(jnp.float32), bias.astype(jnp.float32)).astype(
        jnp.bfloat16
    )
    packed = jnp.dot(
        normed.reshape(-1, features), qkv_w, preferred_element_type=jnp.float32
    ).astype(jnp.bfloat16)
    packed = packed.reshape(images, -1, 3 * features)
    queries = packed[..., :features]
    keys_tok = packed[..., features : 2 * features]
    values_tok = packed[..., 2 * features :]
    onehot = (routed[..., None] == jnp.arange(REGIONS, dtype=jnp.int32)).astype(jnp.bfloat16)
    query_heads = heads_of(queries)
    picked_keys = gather_regions(onehot, keys_tok)
    picked_values = gather_regions(onehot, values_tok)
    score_scale = HEAD_DIM ** (-0.5)
    scores = (
        jnp.einsum(
            "ihrqc,ihrkc->ihrqk", query_heads, picked_keys, preferred_element_type=jnp.float32
        )
        * score_scale
    )
    attn_probs = jax.nn.softmax(scores, axis=-1)
    probs_low = attn_probs.astype(jnp.bfloat16)
    attended = jnp.einsum(
        "ihrqk,ihrkc->ihrqc", probs_low, picked_values, preferred_element_type=jnp.float32
    )
    context = (
        merge_heads(attended)
        + depthwise(values_tok.astype(jnp.float32), lepe_w.astype(jnp.float32))
    ).astype(jnp.bfloat16)
    return (
        base_in,
        mixed_in,
        normed,
        values_tok,
        onehot,
        query_heads,
        picked_keys,
        picked_values,
        attn_probs,
        probs_low,
        context,
    )


def attn_forward(inputs, routed, pos_w, gain, bias, qkv_w, lepe_w, proj_w):
    pieces = attn_pieces(inputs, routed, pos_w, gain, bias, qkv_w, lepe_w)
    mixed_in = pieces[1]
    context = pieces[-1]
    features = inputs.shape[-1]
    result = mixed_in + jnp.dot(
        context.reshape(-1, features), proj_w, preferred_element_type=jnp.float32
    ).reshape(mixed_in.shape)
    return result.astype(jnp.bfloat16)


def attn_backward(inputs, routed, pos_w, gain, bias, qkv_w, lepe_w, proj_w, grad_out):
    (
        base_in,
        mixed_in,
        normed,
        values_tok,
        onehot,
        query_heads,
        picked_keys,
        picked_values,
        attn_probs,
        probs_low,
        context,
    ) = attn_pieces(inputs, routed, pos_w, gain, bias, qkv_w, lepe_w)
    features = inputs.shape[-1]
    grad_rows = grad_out.reshape(-1, features)
    proj_grad = jnp.dot(
        context.reshape(-1, features).T, grad_rows, preferred_element_type=jnp.float32
    )
    grad_context = (
        jnp.dot(grad_rows, proj_w.T, preferred_element_type=jnp.float32)
        .astype(jnp.bfloat16)
        .reshape(mixed_in.shape)
    )
    _, lepe_pull = jax.vjp(depthwise, values_tok.astype(jnp.float32), lepe_w.astype(jnp.float32))
    grad_values_conv, lepe_grad = lepe_pull(grad_context.astype(jnp.float32))
    grad_attended = heads_of(grad_context)
    grad_probs = jnp.einsum(
        "ihrqc,ihrkc->ihrqk", grad_attended, picked_values, preferred_element_type=jnp.float32
    )
    grad_picked_values = jnp.einsum(
        "ihrqk,ihrqc->ihrkc", probs_low, grad_attended, preferred_element_type=jnp.float32
    ).astype(jnp.bfloat16)
    grad_scores = attn_probs * (
        grad_probs - jnp.sum(attn_probs * grad_probs, axis=-1, keepdims=True)
    )
    grad_scores = grad_scores.astype(jnp.bfloat16)
    score_scale = HEAD_DIM ** (-0.5)
    grad_queries = (
        jnp.einsum(
            "ihrqk,ihrkc->ihrqc", grad_scores, picked_keys, preferred_element_type=jnp.float32
        )
        * score_scale
    )
    grad_picked_keys = (
        jnp.einsum(
            "ihrqk,ihrqc->ihrkc", grad_scores, query_heads, preferred_element_type=jnp.float32
        )
        * score_scale
    ).astype(jnp.bfloat16)
    grad_keys = scatter_regions(onehot, grad_picked_keys)
    grad_values = scatter_regions(onehot, grad_picked_values) + grad_values_conv
    grad_packed = jnp.concatenate(
        [merge_heads(grad_queries), grad_keys, grad_values], axis=-1
    ).astype(jnp.bfloat16)
    packed_rows = grad_packed.reshape(-1, 3 * features)
    qkv_grad = jnp.dot(
        normed.reshape(-1, features).T, packed_rows, preferred_element_type=jnp.float32
    )
    grad_normed = (
        jnp.dot(packed_rows, qkv_w.T, preferred_element_type=jnp.float32)
        .astype(jnp.bfloat16)
        .reshape(mixed_in.shape)
    )
    _, norm_pull = jax.vjp(norm_rows, mixed_in, gain.astype(jnp.float32), bias.astype(jnp.float32))
    grad_mixed, gain_grad, bias_grad = norm_pull(grad_normed.astype(jnp.float32))
    grad_mixed = grad_mixed + grad_out.astype(jnp.float32)
    _, pos_pull = jax.vjp(
        lambda signal, kernel: signal + depthwise(signal, kernel),
        base_in,
        pos_w.astype(jnp.float32),
    )
    grad_base, pos_grad = pos_pull(grad_mixed)
    return (
        grad_base.astype(jnp.bfloat16),
        (pos_grad, gain_grad, bias_grad, qkv_grad, lepe_grad, proj_grad),
    )


def mlp_pieces(inputs, gain, bias, fc1_w):
    features = inputs.shape[-1]
    base_rows = inputs.reshape(-1, features).astype(jnp.float32)
    normed = norm_rows(base_rows, gain.astype(jnp.float32), bias.astype(jnp.float32)).astype(
        jnp.bfloat16
    )
    hidden = jnp.dot(normed, fc1_w, preferred_element_type=jnp.float32)
    active = exact_gelu(hidden).astype(jnp.bfloat16)
    return (base_rows, normed, hidden, active)


def mlp_forward(inputs, gain, bias, fc1_w, fc2_w):
    base_rows, normed, hidden, active = mlp_pieces(inputs, gain, bias, fc1_w)
    result = base_rows + jnp.dot(active, fc2_w, preferred_element_type=jnp.float32)
    return result.reshape(inputs.shape).astype(jnp.bfloat16)


def mlp_backward(inputs, gain, bias, fc1_w, fc2_w, grad_out):
    base_rows, normed, hidden, active = mlp_pieces(inputs, gain, bias, fc1_w)
    features = inputs.shape[-1]
    grad_rows = grad_out.reshape(-1, features)
    fc2_grad = jnp.dot(active.T, grad_rows, preferred_element_type=jnp.float32)
    grad_active = jnp.dot(grad_rows, fc2_w.T, preferred_element_type=jnp.float32).astype(
        jnp.bfloat16
    )
    _, gelu_pull = jax.vjp(exact_gelu, hidden)
    grad_hidden = gelu_pull(grad_active.astype(jnp.float32))[0].astype(jnp.bfloat16)
    fc1_grad = jnp.dot(normed.T, grad_hidden, preferred_element_type=jnp.float32)
    grad_normed = jnp.dot(grad_hidden, fc1_w.T, preferred_element_type=jnp.float32).astype(
        jnp.bfloat16
    )
    _, norm_pull = jax.vjp(norm_rows, base_rows, gain.astype(jnp.float32), bias.astype(jnp.float32))
    grad_base, gain_grad, bias_grad = norm_pull(grad_normed.astype(jnp.float32))
    grad_base = grad_base + grad_rows.astype(jnp.float32)
    return (
        grad_base.reshape(inputs.shape).astype(jnp.bfloat16),
        (gain_grad, bias_grad, fc1_grad, fc2_grad),
    )


def per_device(
    tokens,
    routes,
    pos_weight,
    attn_gain,
    attn_bias,
    qkv_weight,
    lepe_weight,
    proj_weight,
    mlp_gain,
    mlp_bias,
    fc1_weight,
    fc2_weight,
    cotangent,
):
    weights = (
        pos_weight,
        attn_gain,
        attn_bias,
        qkv_weight,
        lepe_weight,
        proj_weight,
        mlp_gain,
        mlp_bias,
        fc1_weight,
        fc2_weight,
    )
    layer_count = pos_weight.shape[0]
    segment_total = 2 * layer_count

    def forward_at(number, inputs, routed):
        layer_index = number // 2
        if number % 2 == 0:
            return attn_forward(
                inputs,
                routed[:, layer_index],
                pos_weight[layer_index],
                attn_gain[layer_index],
                attn_bias[layer_index],
                qkv_weight[layer_index],
                lepe_weight[layer_index],
                proj_weight[layer_index],
            )
        return mlp_forward(
            inputs,
            mlp_gain[layer_index],
            mlp_bias[layer_index],
            fc1_weight[layer_index],
            fc2_weight[layer_index],
        )

    def backward_at(number, inputs, routed, grad_out):
        layer_index = number // 2
        if number % 2 == 0:
            grad_in, pieces = attn_backward(
                inputs,
                routed[:, layer_index],
                pos_weight[layer_index],
                attn_gain[layer_index],
                attn_bias[layer_index],
                qkv_weight[layer_index],
                lepe_weight[layer_index],
                proj_weight[layer_index],
                grad_out,
            )
            positions = (0, 1, 2, 3, 4, 5)
        else:
            grad_in, pieces = mlp_backward(
                inputs,
                mlp_gain[layer_index],
                mlp_bias[layer_index],
                fc1_weight[layer_index],
                fc2_weight[layer_index],
                grad_out,
            )
            positions = (6, 7, 8, 9)
        grads = [jnp.zeros(weight.shape[1:], jnp.float32) for weight in weights]
        for position, piece in zip(positions, pieces):
            grads[position] = piece
        return (grad_in, tuple(grads))

    layer_sums = tuple((jnp.zeros(weight.shape[1:], jnp.float32) for weight in weights))
    forwards = [partial(forward_at, number) for number in range(segment_total)]
    backwards = [partial(backward_at, number) for number in range(segment_total)]
    segment_index = lax.axis_index("section")
    segment_count = lax.axis_size("section")
    all_tokens, all_routes, all_cotangent = (
        lax.all_gather(tokens, "section", axis=0, tiled=True),
        lax.all_gather(routes, "section", axis=0, tiled=True),
        lax.all_gather(cotangent, "section", axis=0, tiled=True),
    )
    batches = all_tokens.shape[0]
    tick_count = batches + segment_count - 1
    received = jnp.zeros_like(tokens[0])
    stored = jnp.zeros_like(all_tokens)
    finished = jnp.zeros_like(all_tokens)
    for tick_index in range(tick_count):
        micro_index = tick_index - segment_index
        active = (micro_index >= 0) & (micro_index < batches)
        picked = jnp.clip(micro_index, 0, batches - 1)
        fresh_input = lax.dynamic_index_in_dim(all_tokens, picked, 0, keepdims=False)
        incoming = jnp.where(segment_index == 0, fresh_input, received)
        stored = jnp.where(
            active, lax.dynamic_update_index_in_dim(stored, incoming, picked, 0), stored
        )
        routed = lax.dynamic_index_in_dim(all_routes, picked, 0, keepdims=False)
        outgoing = lax.switch(segment_index, forwards, incoming, routed)
        finished = jnp.where(
            active & (segment_index == segment_count - 1),
            lax.dynamic_update_index_in_dim(finished, outgoing, picked, 0),
            finished,
        )
        if tick_index + 1 < tick_count:
            received = jax.tree.map(
                lambda part, own: part.astype(own.dtype),
                shifted(for_sending(outgoing), "section", 1),
                outgoing,
            )
    received_grad = jnp.zeros_like(tokens[0])
    returned = jnp.zeros_like(all_tokens)
    for tick_index in range(tick_count):
        micro_index = tick_index - (segment_count - 1 - segment_index)
        active = (micro_index >= 0) & (micro_index < batches)
        picked = jnp.clip(micro_index, 0, batches - 1)
        fresh_grad = lax.dynamic_index_in_dim(all_cotangent, picked, 0, keepdims=False)
        incoming = jnp.where(segment_index == segment_count - 1, fresh_grad, received_grad)
        saved_input = lax.dynamic_index_in_dim(stored, picked, 0, keepdims=False)
        routed = lax.dynamic_index_in_dim(all_routes, picked, 0, keepdims=False)
        outgoing, grads = lax.switch(segment_index, backwards, saved_input, routed, incoming)
        layer_sums = tuple(
            (running + jnp.where(active, piece, 0.0) for running, piece in zip(layer_sums, grads))
        )
        returned = jnp.where(
            active & (segment_index == 0),
            lax.dynamic_update_index_in_dim(returned, outgoing, picked, 0),
            returned,
        )
        if tick_index + 1 < tick_count:
            received_grad = jax.tree.map(
                lambda part, own: part.astype(own.dtype),
                shifted(for_sending(outgoing), "section", -1),
                outgoing,
            )
    layer_mask = (jnp.arange(layer_count, dtype=jnp.int32) == segment_index // 2).astype(
        jnp.float32
    )
    grad_sums = tuple(
        (
            layer_mask.reshape((layer_count,) + (1,) * piece.ndim) * piece[None]
            for piece in layer_sums
        )
    )
    outputs = from_root(finished, "section", segment_count - 1)
    output = lax.dynamic_slice_in_dim(outputs, segment_index, 1, 0)
    input_grads = from_root(returned, "section", 0)
    input_grad = lax.dynamic_slice_in_dim(input_grads, segment_index, 1, 0)
    summed = lax.psum(grad_sums, ("section", "dp"))
    return (
        output,
        input_grad,
        summed[0],
        summed[1],
        summed[2],
        summed[3],
        summed[4],
        summed[5],
        summed[6],
        summed[7],
        summed[8],
        summed[9],
    )


def solution(mesh):
    placed = (
        P("section", "dp", None, None),
        P("section", "dp", None, None, None, None),
        P(),
        P(),
        P(),
        P(),
        P(),
        P(),
        P(),
        P(),
        P(),
        P(),
        P("section", "dp", None, None),
    )
    return jax.shard_map(
        per_device,
        mesh=mesh,
        in_specs=placed,
        out_specs=(
            P("section", "dp", None, None),
            P("section", "dp", None, None),
            P(),
            P(),
            P(),
            P(),
            P(),
            P(),
            P(),
            P(),
            P(),
            P(),
        ),
        check_vma=False,
    )
```

profile of v0, /device:TPU:0, one launch (start us, length us, event | category | flops | bytes accessed | tf_op | source)
XLA Modules:
  0.0 1267.9 jit_solution(9620349906098358078)
XLA Ops:
  8.0 9.9 all_gather.10
  17.9 10.0 all_gather.9
  28.0 23.8 %conditional.14 = (bf16[1,196,256]{2,1,0:T(8,128)(2,1)}, bf16[1,1,196,256]{3,2,1,0:T(8,128)(2,1)S(1)}) conditional(s32[]{:T(128)} %clamp.2, (bf16[1,196,256]{2,1,0:T(8,128)(2,1)S(1)}, bf16[2,9,256]{2,0,1:T(2,128)(2,1)}, bf16[2,256]{1,0:T(2,128)(2,1)}, bf16[2,256]{1,0:T(2,128)(2,1)}, bf16[2,256,768]{2,1,0:T(8,128)(2,1)}, ...), branch_computations={%region_0.5_spmd, %region_5.8_spmd, %region_8.13_spmd, %region_13.... | conditional | flops 164678336 | bytes 18774716 | solution.py:403
  32.4 4.7 multiply_add_fusion
  53.4 11.1 all_gather.11
  66.1 27.4 %conditional.15 = (bf16[1,196,256]{2,1,0:T(8,128)(2,1)}, bf16[1,1,196,256]{3,2,1,0:T(8,128)(2,1)S(1)}) conditional(s32[]{:T(128)} %clamp.2, (bf16[1,196,256]{2,1,0:T(8,128)(2,1)S(1)}, bf16[2,9,256]{2,0,1:T(2,128)(2,1)S(1)}, bf16[2,256]{1,0:T(2,128)(2,1)S(1)}, bf16[2,256]{1,0:T(2,128)(2,1)S(1)}, ...), branch_computations={%region_16.21_spmd, %region_21.24_spmd, %region_24.29_spmd, %regio... | conditional | flops 164678336 | bytes 15383228 | solution.py:403
  68.7 4.7 multiply_add_fusion.4
  83.5 3.4 fusion.3202
  98.3 30.5 %conditional.16 = (bf16[1,196,256]{2,1,0:T(8,128)(2,1)}, bf16[1,1,196,256]{3,2,1,0:T(8,128)(2,1)S(1)}) conditional(s32[]{:T(128)} %clamp.2, (bf16[1,196,256]{2,1,0:T(8,128)(2,1)S(1)}, bf16[2,9,256]{2,0,1:T(2,128)(2,1)S(1)}, bf16[2,256]{1,0:T(2,128)(2,1)S(1)}, bf16[2,256]{1,0:T(2,128)(2,1)S(1)}, ...), branch_computations={%region_32.37_spmd, %region_37.40_spmd, %region_40.45_spmd, %regio... | conditional | flops 164678336 | bytes 15383228 | solution.py:403
  103.8 4.7 multiply_add_fusion.8
  118.6 3.4 fusion.3210
  133.6 30.3 %conditional.17 = (bf16[1,196,256]{2,1,0:T(8,128)(2,1)}, bf16[1,1,196,256]{3,2,1,0:T(8,128)(2,1)S(1)}) conditional(s32[]{:T(128)} %clamp.2, (bf16[1,196,256]{2,1,0:T(8,128)(2,1)S(1)}, bf16[2,9,256]{2,0,1:T(2,128)(2,1)S(1)}, bf16[2,256]{1,0:T(2,128)(2,1)S(1)}, bf16[2,256]{1,0:T(2,128)(2,1)S(1)}, ...), branch_computations={%region_48.53_spmd, %region_53.56_spmd, %region_56.61_spmd, %regio... | conditional | flops 164678336 | bytes 15383228 | solution.py:403
  139.1 4.7 multiply_add_fusion.12
  153.9 3.4 fusion.3218
  168.7 30.5 %conditional.18 = (bf16[1,196,256]{2,1,0:T(8,128)(2,1)}, bf16[1,1,196,256]{3,2,1,0:T(8,128)(2,1)S(1)}) conditional(s32[]{:T(128)} %clamp.2, (bf16[1,196,256]{2,1,0:T(8,128)(2,1)S(1)}, bf16[2,9,256]{2,0,1:T(2,128)(2,1)S(1)}, bf16[2,256]{1,0:T(2,128)(2,1)S(1)}, bf16[2,256]{1,0:T(2,128)(2,1)S(1)}, ...), branch_computations={%region_64.69_spmd, %region_69.72_spmd, %region_72.77_spmd, %regio... | conditional | flops 164678336 | bytes 15383228 | solution.py:403
  174.4 4.7 multiply_add_fusion.16
  189.2 3.4 fusion.3226
  199.2 7.9 collective-permute-start.4
  210.6 27.4 %conditional.19 = (bf16[1,196,256]{2,1,0:T(8,128)(2,1)}, bf16[1,1,196,256]{3,2,1,0:T(8,128)(2,1)S(1)}) conditional(s32[]{:T(128)} %clamp.2, (bf16[1,196,256]{2,1,0:T(8,128)(2,1)S(1)}, bf16[2,9,256]{2,0,1:T(2,128)(2,1)S(1)}, bf16[2,256]{1,0:T(2,128)(2,1)S(1)}, bf16[2,256]{1,0:T(2,128)(2,1)S(1)}, ...), branch_computations={%region_80.85_spmd, %region_85.88_spmd, %region_88.93_spmd, %regio... | conditional | flops 164678336 | bytes 15383228 | solution.py:403
  213.0 4.7 multiply_add_fusion.20
  227.8 3.4 fusion.3234
  238.0 12.8 %collective-permute-start.5 = (bf16[1,196,256]{2,1,0:T(8,128)(2,1)}, bf16[1,196,256]{2,1,0:T(8,128)(2,1)S(1)}, u32[]{:S(2)}, u32[]{:S(2)}) collective-permute-start(bf16[1,196,256]{2,1,0:T(8,128)(2,1)} %get-tuple-element.2019), channel_id=1, source_target_pairs={{0,8},{8,16},{16,24},{1,9},{9,17},{17,25},{2,10},{10,18},{18,26},{... | collective-permute-start | bytes 301064 | tf_op jit(solution)/shard_map/ppermute | solution.py:27
  255.1 25.6 %conditional.20 = (bf16[1,1,196,256]{3,2,1,0:T(8,128)(2,1)S(1)}) conditional(s32[]{:T(128)} %clamp.2, (bf16[1,196,256]{2,1,0:T(8,128)(2,1)S(1)}, bf16[2,9,256]{2,0,1:T(2,128)(2,1)S(1)}, bf16[2,256]{1,0:T(2,128)(2,1)S(1)}, bf16[2,256]{1,0:T(2,128)(2,1)S(1)}, bf16[2,256,768]{2,1,0:T(8,128)(2,1)S(1)}, ...), branch_computations={%region_96.101_spmd, %region_101.104_spmd, %region_104.109_spmd, %... | conditional | flops 164678336 | bytes 15182516 | solution.py:403
  257.5 4.7 multiply_add_fusion.24
  272.3 3.4 fusion.3242
  281.6 79.9 %conditional.21 = (bf16[1,196,256]{2,1,0:T(8,128)(2,1)}, f32[9,256]{1,0:T(8,128)S(1)}, f32[256]{0:T(256)S(1)}, f32[256]{0:T(256)S(1)}, f32[256,768]{1,0:T(8,128)...) conditional(s32[]{:T(128)} %clamp.2, ...), branch_computations={%region_113.157_spmd, %region_157.164_spmd, %region_164.208_spmd, ... | conditional | flops 399954272 | bytes 58117692 | solution.py:425
  302.0 3.6 fusion.3250
  305.6 3.5 convolution_bitcast_fusion.28
  315.8 3.4 convolution_convert_fusion.42
  363.0 5.4 collective-permute-done.6
  369.4 82.6 %conditional.22 = (bf16[1,196,256]{2,1,0:T(8,128)(2,1)}, f32[9,256]{1,0:T(8,128)S(1)}, f32[256]{0:T(256)}, f32[256]{0:T(256)}, f32[256,768]{1,0:T(8,128)S(1)}, /...) conditional(s32[]{:T(128)} %clamp.2, ...), branch_computations={%region_215.259_spmd, %region_259.266_spmd, %region_266.310_spmd, ... | conditional | flops 399954272 | bytes 58234220 | solution.py:425
  386.8 3.6 fusion.3258
  390.4 3.5 convolution_bitcast_fusion.32
  401.2 3.4 convolution_convert_fusion.58
  411.5 3.0 multiply_convert_fusion.8
  454.9 3.9 collective-permute-done.7
  459.8 84.3 %conditional.23 = (bf16[1,196,256]{2,1,0:T(8,128)(2,1)}, f32[9,256]{1,0:T(8,128)S(1)}, f32[256]{0:T(256)}, f32[256]{0:T(256)}, f32[256,768]{1,0:T(8,128)S(1)}, /...) conditional(s32[]{:T(128)} %clamp.2, ...), branch_computations={%region_317.361_spmd, %region_361.368_spmd, %region_368.412_spmd, ... | conditional | flops 399954272 | bytes 58234220 | solution.py:425
  477.0 3.6 fusion.3266
  480.6 3.5 convolution_bitcast_fusion.36
  491.4 3.4 convolution_convert_fusion.74
  547.1 3.9 collective-permute-done.8
  551.9 82.7 %conditional.24 = (bf16[1,196,256]{2,1,0:T(8,128)(2,1)}, f32[9,256]{1,0:T(8,128)S(1)}, f32[256]{0:T(256)S(1)}, f32[256]{0:T(256)}, f32[256,768]{1,0:T(8,128)S(1)...) conditional(s32[]{:T(128)} %clamp.2, ...), branch_computations={%region_419.463_spmd, %region_463.470_spmd, %region_470.514_spmd, ... | conditional | flops 399954272 | bytes 58234220 | solution.py:425
  569.0 3.6 fusion.3274
  572.7 3.5 convolution_bitcast_fusion.40
  583.5 3.4 convolution_convert_fusion.90
  637.6 3.9 collective-permute-done.9
  642.5 82.5 %conditional.25 = (bf16[1,196,256]{2,1,0:T(8,128)(2,1)}, f32[9,256]{1,0:T(8,128)S(1)}, f32[256]{0:T(256)}, f32[256]{0:T(256)}, f32[256,768]{1,0:T(8,128)S(1)}, /...) conditional(s32[]{:T(128)} %clamp.2, ...), branch_computations={%region_521.565_spmd, %region_565.572_spmd, %region_572.616_spmd, ... | conditional | flops 399954272 | bytes 58234220 | solution.py:425
  659.8 3.7 fusion.3282
  663.5 3.5 convolution_bitcast_fusion.44
  674.3 3.4 convolution_convert_fusion.106
  728.0 3.9 collective-permute-done.10
  732.9 82.5 %conditional.26 = (bf16[1,196,256]{2,1,0:T(8,128)(2,1)}, f32[9,256]{1,0:T(8,128)S(1)}, f32[256]{0:T(256)}, f32[256]{0:T(256)}, f32[256,768]{1,0:T(8,128)S(1)}, /...) conditional(s32[]{:T(128)} %clamp.2, ...), branch_computations={%region_623.667_spmd, %region_667.674_spmd, %region_674.718_spmd, ... | conditional | flops 399954272 | bytes 58234220 | solution.py:425
  750.0 3.6 fusion.3290
  753.6 3.5 convolution_bitcast_fusion.48
  764.4 3.4 convolution_convert_fusion.122
  818.3 3.9 collective-permute-done.11
  823.2 75.5 %conditional.27 = (f32[9,256]{1,0:T(8,128)S(1)}, f32[256]{0:T(256)S(1)}, f32[256]{0:T(256)S(1)}, f32[256,768]{1,0:T(8,128)S(1)}, f32[25,256]{1,0:T(8,128)S(1)}, ...) conditional(s32[]{:T(128)} %clamp.2, ...), branch_computations={%region_725.769_spmd, %region_769.776_spmd, %region_776.820_spmd, ... | conditional | flops 399954272 | bytes 56737500 | solution.py:425
  839.0 3.7 fusion.3298
  842.6 3.5 convolution_bitcast_fusion.52
  852.8 3.4 convolution_convert_fusion.138
  863.1 3.0 multiply_convert_fusion.48
  919.7 39.9 %all-reduce.1019.cloned.1.call-done = (bf16[4,1,196,256]{3,2,1,0:T(8,128)(2,1)}, bf16[4,1,196,256]{3,2,1,0:T(8,128)(2,1)}) async-done(((bf16[4,1,196,256]{3,2,1,0:T(8,128)(2,1)}, bf16[4,1,196,256]{3,2,1,0:T(8,128)(2,1)}), (bf16[4,1,196,256]{3,2,1,0:T(8,128)(2,1)}, bf16[4,1,196,256]{3,2,1,0:T(8,128)(2,1)})) %all-reduce.1019.cloned.1.call-update) | async-done | bytes 802832 | tf_op jit(solution)/shard_map/psum | solution.py:32
  961.2 129.2 %all-reduce.1015.cloned.1.call-done = (f32[2,9,256]{2,0,1:T(2,128)}, f32[2,256]{1,0:T(2,128)}, f32[2,256]{1,0:T(2,128)}, f32[2,25,256]{2,0,1:T(2,128)}, f32[2,256]{1,0:T(2,128)}, /*index=5*/f32[2,256]{1,0:T(2,128)}) async-done(((f32[2,9,256]{2,0,1:T(2,128)}, f32[2,256]{1,0:T(2,128)}, f32[2,256]{1,0:T(2,128)}, f32[2,25,256]{2,0,1:T(2,128)}, f32[2,256]{1,0:T(2,128)}, /*index=5*/f32[2,256]{1,0:T(2,128)}), ...) | async-done | bytes 77840 | tf_op jit(solution)/shard_map/psum | solution.py:453
  1090.4 159.2 %all-reduce.1017.cloned.1.call-done = (f32[2,256,768]{2,1,0:T(8,128)}, f32[2,256,256]{2,1,0:T(8,128)}, f32[2,256,768]{2,1,0:T(8,128)}, f32[2,768,256]{2,1,0:T(8,128)}) async-done(((f32[2,256,768]{2,1,0:T(8,128)}, f32[2,256,256]{2,1,0:T(8,128)}, f32[2,256,768]{2,1,0:T(8,128)}, f32[2,768,256]{2,1,0:T(8,128)}), (f32[2,256,768]{2,1,0:T(8,128)}, f32[2,256,256]{2,1,0:T(8,128)}, f32[2,256,768]{2,1,0:T(8,128)}, ...) | async-done | bytes 5242896 | tf_op jit(solution)/shard_map/psum | solution.py:453
  (2689 shorter events, 546.7 us)
Async XLA Ops:
  7.2 952.4 %all-reduce.1019.cloned.1.call-start = ((), (), s32[]{:S(2)}) async-start(), calls=%async_computation.2 | async-start | bytes 1638400 | tf_op jit(solution)/shard_map/psum | solution.py:32
  27.9 38.1 %copy-start.91 = (bf16[4,1,196,256]{3,2,1,0:T(8,128)(2,1)}, bf16[4,1,196,256]{3,2,1,0:T(8,128)(2,1)S(1)}, u32[]{:S(2)}) copy-start(bf16[4,1,196,256]{3,2,1,0:T(8,128)(2,1)S(1)} %all_gather.9) | copy-start | bytes 1204228
  27.9 25.5 %copy-start.310 = (bf16[1,1,196,256]{3,2,1,0:T(8,128)(2,1)S(1)}, bf16[1,1,196,256]{3,2,1,0:T(8,128)(2,1)}, u32[]{:S(2)}) copy-start(bf16[1,1,196,256]{3,2,1,0:T(8,128)(2,1)} %param.81) | copy-start | bytes 301060
  51.8 14.3 %copy-start = (bf16[2,256,768]{2,1,0:T(8,128)(2,1)S(1)}, bf16[2,256,768]{2,1,0:T(8,128)(2,1)}, u32[]{:S(2)}) copy-start(bf16[2,256,768]{2,1,0:T(8,128)(2,1)} %param.74) | copy-start | bytes 2359300
  51.8 14.3 %copy-start.8 = (bf16[2,25,256]{2,0,1:T(2,128)(2,1)S(1)}, bf16[2,25,256]{2,0,1:T(2,128)(2,1)}, u32[]{:S(2)}) copy-start(bf16[2,25,256]{2,0,1:T(2,128)(2,1)} %param.75) | copy-start | bytes 76804
  51.8 14.3 %copy-start.9 = (bf16[2,256,256]{2,1,0:T(8,128)(2,1)S(1)}, bf16[2,256,256]{2,1,0:T(8,128)(2,1)}, u32[]{:S(2)}) copy-start(bf16[2,256,256]{2,1,0:T(8,128)(2,1)} %param.76) | copy-start | bytes 786436
  51.8 14.3 %copy-start.13 = (bf16[2,9,256]{2,0,1:T(2,128)(2,1)S(1)}, bf16[2,9,256]{2,0,1:T(2,128)(2,1)}, u32[]{:S(2)}) copy-start(bf16[2,9,256]{2,0,1:T(2,128)(2,1)} %param.71) | copy-start | bytes 27652
  51.8 14.3 %copy-start.190 = (bf16[2,256]{1,0:T(2,128)(2,1)S(1)}, bf16[2,256]{1,0:T(2,128)(2,1)}, u32[]{:S(2)}) copy-start(bf16[2,256]{1,0:T(2,128)(2,1)} %param.72) | copy-start | bytes 3076
  51.8 14.3 %copy-start.191 = (bf16[2,256]{1,0:T(2,128)(2,1)S(1)}, bf16[2,256]{1,0:T(2,128)(2,1)}, u32[]{:S(2)}) copy-start(bf16[2,256]{1,0:T(2,128)(2,1)} %param.73) | copy-start | bytes 3076
  51.8 14.2 %copy-start.192 = (bf16[2,256]{1,0:T(2,128)(2,1)S(1)}, bf16[2,256]{1,0:T(2,128)(2,1)}, u32[]{:S(2)}) copy-start(bf16[2,256]{1,0:T(2,128)(2,1)} %param.77) | copy-start | bytes 3076
  51.8 14.2 %copy-start.193 = (bf16[2,256]{1,0:T(2,128)(2,1)S(1)}, bf16[2,256]{1,0:T(2,128)(2,1)}, u32[]{:S(2)}) copy-start(bf16[2,256]{1,0:T(2,128)(2,1)} %param.78) | copy-start | bytes 3076
  51.9 14.1 %collective-permute-start = (bf16[1,196,256]{2,1,0:T(8,128)(2,1)}, bf16[1,196,256]{2,1,0:T(8,128)(2,1)S(1)}, u32[]{:S(2)}, u32[]{:S(2)}) collective-permute-start(bf16[1,196,256]{2,1,0:T(8,128)(2,1)} %get-tuple-element.2009), channel_id=1, source_target_pairs={{0,8},{8,16},{16,24},{1,9},{9,17},{17,25},{2,10},{10,18},{18,26},{... | collective-permute-start | bytes 301064 | tf_op jit(solution)/shard_map/ppermute | solution.py:27
  93.5 3.8 collective-permute-start.1
  128.8 3.8 collective-permute-start.2
  163.9 3.8 collective-permute-start.3
  199.2 10.5 collective-permute-start.4
  238.0 15.4 %collective-permute-start.5 = (bf16[1,196,256]{2,1,0:T(8,128)(2,1)}, bf16[1,196,256]{2,1,0:T(8,128)(2,1)S(1)}, u32[]{:S(2)}, u32[]{:S(2)}) collective-permute-start(bf16[1,196,256]{2,1,0:T(8,128)(2,1)} %get-tuple-element.2019), channel_id=1, source_target_pairs={{0,8},{8,16},{16,24},{1,9},{9,17},{17,25},{2,10},{10,18},{18,26},{... | collective-permute-start | bytes 301064 | tf_op jit(solution)/shard_map/ppermute | solution.py:27
  255.1 25.7 %copy-start.12 = (bf16[1,196,256]{2,1,0:T(8,128)(2,1)S(1)}, bf16[1,196,256]{2,1,0:T(8,128)(2,1)}, u32[]{:S(2)}) copy-start(bf16[1,196,256]{2,1,0:T(8,128)(2,1)} %select_bitcast_fusion) | copy-start | bytes 301060
  361.5 7.8 copy-start.1506
  361.5 7.8 copy-start.311
  361.6 7.8 copy-start.1487
  361.6 7.8 copy-start.1498
  361.6 7.8 copy-start.1504
  361.6 7.8 copy-start.65
  361.6 7.8 copy-start.77
  361.6 7.8 copy-start.79
  361.6 7.8 copy-start.307
  361.6 6.8 collective-permute-start.6
  369.3 90.4 %copy-start.7 = (bf16[1,196,256]{2,1,0:T(8,128)(2,1)S(1)}, bf16[1,196,256]{2,1,0:T(8,128)(2,1)}, u32[]{:S(2)}) copy-start(bf16[1,196,256]{2,1,0:T(8,128)(2,1)} %get-tuple-element.5631) | copy-start | bytes 301060
  370.5 10.5 copy-start.287
  452.0 6.8 collective-permute-start.7
  459.7 92.1 %copy-start.6 = (bf16[1,196,256]{2,1,0:T(8,128)(2,1)S(1)}, bf16[1,196,256]{2,1,0:T(8,128)(2,1)}, u32[]{:S(2)}) copy-start(bf16[1,196,256]{2,1,0:T(8,128)(2,1)} %get-tuple-element.5630) | copy-start | bytes 301060
  460.9 10.5 copy-start.291
  544.2 6.8 collective-permute-start.8
  551.9 90.5 %copy-start.5 = (bf16[1,196,256]{2,1,0:T(8,128)(2,1)S(1)}, bf16[1,196,256]{2,1,0:T(8,128)(2,1)}, u32[]{:S(2)}) copy-start(bf16[1,196,256]{2,1,0:T(8,128)(2,1)} %get-tuple-element.5629) | copy-start | bytes 301060
  553.0 10.5 copy-start.295
  634.7 7.8 copy-start.1500
  634.7 7.8 copy-start.1518
  634.7 7.8 copy-start.1516
  634.7 7.8 copy-start.71
  634.7 7.8 copy-start.85
  634.7 7.8 copy-start.314
  634.7 6.8 collective-permute-start.9
  642.4 90.4 %copy-start.4 = (bf16[1,196,256]{2,1,0:T(8,128)(2,1)S(1)}, bf16[1,196,256]{2,1,0:T(8,128)(2,1)}, u32[]{:S(2)}) copy-start(bf16[1,196,256]{2,1,0:T(8,128)(2,1)} %get-tuple-element.5628) | copy-start | bytes 301060
  643.6 10.5 copy-start.299
  725.0 7.8 copy-start.1520
  725.1 6.8 collective-permute-start.10
  732.8 90.4 %copy-start.3 = (bf16[1,196,256]{2,1,0:T(8,128)(2,1)S(1)}, bf16[1,196,256]{2,1,0:T(8,128)(2,1)}, u32[]{:S(2)}) copy-start(bf16[1,196,256]{2,1,0:T(8,128)(2,1)} %get-tuple-element.5627) | copy-start | bytes 301060
  734.0 10.5 copy-start.303
  815.4 7.8 copy-start.1524
  815.4 7.8 copy-start.1526
  815.4 7.8 copy-start.75
  815.4 7.8 copy-start.88
  815.4 7.8 copy-start.89
  815.5 7.8 copy-start.316
  815.5 6.8 collective-permute-start.11
  823.2 81.5 %copy-start.308 = (f32[25,256]{1,0:T(8,128)S(1)}, f32[25,256]{1,0:T(8,128)}, u32[]{:S(2)}) copy-start(f32[25,256]{1,0:T(8,128)} %copy-done.307) | copy-start | bytes 76804
  823.2 81.4 %copy-start.309 = (f32[25,256]{1,0:T(8,128)S(1)}, f32[25,256]{1,0:T(8,128)}, u32[]{:S(2)}) copy-start(f32[25,256]{1,0:T(8,128)} %get-tuple-element.2062) | copy-start | bytes 76804
  851.8 23.2 %copy-start.205 = (bf16[196,256]{1,0:T(8,128)(2,1)}, bf16[196,256]{1,0:T(8,128)(2,1)S(1)}, u32[]{:S(2)}) copy-start(bf16[196,256]{1,0:T(8,128)(2,1)S(1)} %concatenate.162) | copy-start | bytes 301060 | tf_op jit(solution)/shard_map/cond
  898.8 8.0 copy-start.63
  898.8 8.0 copy-start.80
  898.8 8.0 copy-start.84
  910.6 179.8 %all-reduce.1015.cloned.1.call-start = ((), (), s32[]{:S(2)}) async-start(), calls=%async_computation | async-start | bytes 155648 | tf_op jit(solution)/shard_map/psum | solution.py:453
  918.7 330.9 %all-reduce.1017.cloned.1.call-start = ((), (), s32[]{:S(2)}) async-start(), calls=%async_computation.1 | async-start | bytes 10485760 | tf_op jit(solution)/shard_map/psum | solution.py:453
  (754 other events, 2151.0 us)
Sparse Core Ops, SparseCore 0:
  910.7 48.8 all-reduce.1018
  968.3 122.0 all-reduce.1014
  1098.7 150.8 all-reduce.1016
where the time goes:
time: 1280 us; the launch traced here: 1270 us
  waiting for transfers between devices  366 us (29%)
  local copies, waits for them, and re-layouts  264 us (21%)
  matrix products  210 us (16%)
  other arithmetic  180 us (14%)
  loops' own time  167 us (13%)
  starting transfers between devices  33.9 us (3%)
  blocking collectives  30.9 us (2%)
  between operations  15.9 us (1%)
    psum x2, waiting for transfers between devices, per_device(): summed = lax.psum(grad_sums, ('section', 'dp'))  288 us
    another operation x7, loops' own time, per_device(): lax.switch(segment_index, backwards, saved_input, routed, incoming)  153 us
    another operation x122, local copies, waits for them, and re-layouts  91.6 us
    add x28, other arithmetic, depthwise(): summed + padded[:, row_tap:row_tap + SIDE, col_tap:col_tap + SIDE, :] * k...  51.6 us
    sub x14, matrix products, attn_pieces(): attn_probs = jax.nn.softmax(scores, axis=-1)  48.3 us
    dot_general x14, matrix products, attn_pieces(): jnp.einsum('ihrqk,ihrkc->ihrqc', probs_low, picked_values, preferred_elem...  40.9 us
    psum x1, waiting for transfers between devices, from_root(): return lax.psum(block, axis)  39.9 us
    ppermute x12, waiting for transfers between devices, shifted(): return lax.ppermute(block, axis, route)  37.4 us
  transfers between devices with their start and end apart: 15, of which 14 were waited for; matrix products, arithmetic and copies ran while one was open for 1% of the time, Pallas kernels for 0%

commit v1 on v0

v1 whole, which is shorter than its diff:
```python
from functools import partial
import math

import jax
import jax.numpy as jnp
from jax import lax
from jax.experimental import pallas as pl
from jax.experimental.pallas import tpu as pltpu
from jax.sharding import PartitionSpec as P

F32 = jnp.float32
BF16 = jnp.bfloat16
EPS = 1e-06
HEADS = 8
SIDE = 14
WIDE = 16
TOKS = SIDE * SIDE
ROWS = SIDE * WIDE
FULL = 256
D = 256
HD = 32
REGIONS = 49
TOPK = 4
BLOCKED = -1e30
LOG2E = 1.4426950408889634


def nn(a, b):
    return lax.dot_general(a, b, (((1,), (0,)), ((), ())), preferred_element_type=F32)


def nt(a, b):
    return lax.dot_general(a, b, (((1,), (1,)), ((), ())), preferred_element_type=F32)


def tn(a, b):
    return lax.dot_general(a, b, (((0,), (0,)), ((), ())), preferred_element_type=F32)


def iota(shape, dim):
    return lax.broadcasted_iota(jnp.int32, shape, dim)


def region_of(t):
    return (t >> 5) * (SIDE // 2) + ((t & 15) >> 1)


def valid(t):
    return ((t & 15) < SIDE) & (t < ROWS)


def keep_rows():
    return valid(iota((ROWS, 1), 0))


def norm_parts(v):
    mean = jnp.sum(v, axis=-1, keepdims=True) * (1.0 / D)
    cen = v - mean
    var = jnp.sum(cen * cen, axis=-1, keepdims=True) * (1.0 / D)
    rstd = lax.rsqrt(var + EPS)
    return cen * rstd, rstd


def shifted_into(s_ref, x, extent):
    radius = extent // 2
    for b in range(extent):
        away = b - radius
        s_ref[b, pl.ds(32, ROWS), :] = x if away == 0 else pltpu.roll(x, (-away) % ROWS, 0)


CH = 112


def conv_from(s_ref, taps, extent, flip, base, out_ref):
    radius = extent // 2
    for half in range(2):
        lanes = pl.ds(half * 128, 128)
        for c in range(ROWS // CH):
            acc = None
            for a in range(extent):
                for b in range(extent):
                    tap = a * extent + b
                    if flip:
                        tap = extent * extent - 1 - tap
                    part = s_ref[b, pl.ds(32 + c * CH + 16 * (a - radius), CH), lanes]
                    part = part * taps[pl.ds(tap, 1), lanes]
                    acc = part if acc is None else acc + part
            rows = pl.ds(c * CH, CH)
            if base is not None:
                acc = acc + base[rows, lanes]
            out_ref[rows, lanes] = acc


def conv_taps_grad(s_ref, d_ref, extent, store):
    radius = extent // 2
    for half in range(2):
        lanes = pl.ds(half * 128, 128)
        sums = [None] * (extent * extent)
        for c in range(ROWS // CH):
            d = d_ref[pl.ds(c * CH, CH), lanes]
            for a in range(extent):
                for b in range(extent):
                    part = s_ref[b, pl.ds(32 + c * CH + 16 * (a - radius), CH), lanes] * d
                    part = jnp.sum(part.reshape(CH // 8, 8, 128), axis=0)
                    tap = a * extent + b
                    sums[tap] = part if sums[tap] is None else sums[tap] + part
        for tap, s in enumerate(sums):
            store(tap, lanes, jnp.sum(s, axis=0, keepdims=True))


def half_lanes_mask(h):
    lane = iota((1, 128), 1)
    lo = (h % 4) * HD
    return (lane >= lo) & (lane < lo + HD)


def gelu_pair(x):
    cdf = 0.5 * (1.0 + lax.erf(x * (2.0**-0.5)))
    pdf = jnp.exp2(x * x * (-0.5 * LOG2E)) * (1.0 / math.sqrt(2.0 * math.pi))
    return x * cdf, cdf + x * pdf


class K:
    pass


def attn_fwd(l, k):
    x = k.x[...]
    shifted_into(k.sx.at[l], x, 3)
    conv_from(k.sx.at[l], k.posf.at[l], 3, False, k.x, k.tmp)
    mixed = k.tmp[...]
    xhat, rstd = norm_parts(mixed)
    k.a_xhat[l] = xhat
    k.a_rstd[l] = rstd
    gain = k.againf[pl.ds(l, 1), :]
    bias = k.abiasf[pl.ds(l, 1), :]
    normed = jnp.where(keep_rows(), xhat * gain + bias, 0.0).astype(BF16)
    k.a_normed[l] = normed
    packed = nn(normed, k.qkv[l]).astype(BF16)
    q = packed[:, :D]
    key = packed[:, D : 2 * D]
    val = packed[:, 2 * D :]
    k.key[l] = key
    k.val[l] = val
    zpad = jnp.zeros((FULL - ROWS, D), BF16)
    k.qT[l] = jnp.concatenate([q, zpad], 0).T
    k.kT[l] = jnp.concatenate([key, zpad], 0).T
    k.vT[l] = jnp.concatenate([val, zpad], 0).T
    shifted_into(k.sv.at[l], val.astype(F32), 5)
    conv_from(k.sv.at[l], k.lepef.at[l], 5, False, None, k.tmp2)
    ekey = k.ekey[...]
    eqT = k.eqT[...]
    c = HD**-0.5 * LOG2E
    for half in range(2):
        lanes = slice(half * 128, half * 128 + 128)
        rhs = jnp.concatenate([k.qT[l, lanes, :], eqT], 0)
        khalf = k.key[l, :, lanes]
        for hh in range(4):
            h = half * 4 + hh
            blocked = nn(ekey, k.open[l * HEADS + h]).astype(BF16)
            lhs = jnp.concatenate([jnp.where(half_lanes_mask(h), khalf, jnp.zeros_like(khalf)), blocked], 1)
            s = nn(lhs, rhs)
            m = jnp.max(s, axis=0, keepdims=True)
            e = jnp.exp2((s - m) * c)
            r = 1.0 / jnp.sum(e, axis=0, keepdims=True)
            p = e * r
            k.p[l * HEADS + h] = p
            pb = p.astype(BF16)
            k.pb[l * HEADS + h, :ROWS] = pb
            k.oT[pl.ds(h * HD, HD), :] = nn(k.vT[l, pl.ds(h * HD, HD), :], k.pb[l * HEADS + h])
    ctx = (k.oT[...].T[:ROWS] + k.tmp2[...]).astype(BF16)
    k.ctx[l] = ctx
    res = k.tmp[...] + nn(ctx, k.proj[l])
    k.x[...] = jnp.where(keep_rows(), res, 0.0).astype(BF16).astype(F32)


def mlp_fwd(l, k):
    x = k.x[...]
    xhat, rstd = norm_parts(x)
    k.m_xhat[l] = xhat
    k.m_rstd[l] = rstd
    normed = (xhat * k.mgainf[pl.ds(l, 1), :] + k.mbiasf[pl.ds(l, 1), :]).astype(BF16)
    k.m_normed[l] = normed
    hidden = nn(normed, k.fc1[l])
    act, slope = gelu_pair(hidden)
    act = act.astype(BF16)
    k.act[l] = act
    k.slope[l] = slope
    res = x + nn(act, k.fc2[l])
    k.x[...] = jnp.where(keep_rows(), res, 0.0).astype(BF16).astype(F32)


def norm_bwd(dy, xhat, rstd, gain, store_gain, store_bias):
    store_gain(jnp.sum(dy * xhat, axis=0, keepdims=True))
    store_bias(jnp.sum(dy, axis=0, keepdims=True))
    dg = dy * gain
    m1 = jnp.sum(dg, axis=-1, keepdims=True) * (1.0 / D)
    m2 = jnp.sum(dg * xhat, axis=-1, keepdims=True) * (1.0 / D)
    return rstd * (dg - m1 - xhat * m2)


def mlp_bwd(l, k):
    g = k.g[...]
    gb = g.astype(BF16)
    k.store("fc2", l, tn(k.act[l], gb))
    dact = nt(gb, k.fc2[l]).astype(BF16).astype(F32)
    dhid = (k.slope[l] * dact).astype(BF16)
    k.store("fc1", l, tn(k.m_normed[l], dhid))
    dn = nt(dhid, k.fc1[l]).astype(BF16).astype(F32)
    dx = norm_bwd(
        dn,
        k.m_xhat[l],
        k.m_rstd[l],
        k.mgainf[pl.ds(l, 1), :],
        lambda v: k.store_row("mgain", l, 0, slice(None), v),
        lambda v: k.store_row("mbias", l, 0, slice(None), v),
    )
    k.g[...] = (dx + g).astype(BF16).astype(F32)


def attn_bwd_start(l, k):
    g = k.g[...]
    gb = g.astype(BF16)
    k.store("proj", l, tn(k.ctx[l], gb))
    dctx = nt(gb, k.proj[l]).astype(BF16)
    dctx32 = dctx.astype(F32)
    k.tmp[...] = dctx32
    zpad = jnp.zeros((FULL - ROWS, D), BF16)
    k.dcT[...] = jnp.concatenate([dctx, zpad], 0).T
    shifted_into(k.sd, dctx32, 5)


def attn_bwd_lepe(l, k):
    conv_taps_grad(k.sv.at[l], k.tmp, 5, lambda tap, lanes, v: k.store_row("lepe", l, tap, lanes, v))


def attn_bwd_conv(l, k):
    conv_from(k.sd, k.lepef.at[l], 5, True, None, k.tmp2)


def attn_bwd_heads(l, k, half):
    scale = HD**-0.5
    lanes = slice(half * 128, half * 128 + 128)
    vhalf = k.val[l, :, lanes]
    rhs = k.dcT[lanes, :]
    for hh in range(4):
        h = half * 4 + hh
        hrows = pl.ds(h * HD, HD)
        dp = nn(jnp.where(half_lanes_mask(h), vhalf, jnp.zeros_like(vhalf)), rhs)
        k.dvT[hrows, :] = nt(k.dcT[hrows, :], k.pb[l * HEADS + h])
        p = k.p[l * HEADS + h]
        pd = p * dp
        ds = pd - p * jnp.sum(pd, axis=0, keepdims=True)
        k.ds[hh % 2, :ROWS] = ds.astype(BF16)
        dsb = k.ds[hh % 2]
        k.dqT[hrows, :] = nn(k.kT[l, hrows, :], dsb) * scale
        k.dkT[hrows, :] = nt(k.qT[l, hrows, :], dsb) * scale
    dq = k.dqT[lanes, :].T[:ROWS].astype(BF16)
    dk = k.dkT[lanes, :].T[:ROWS].astype(BF16)
    dv = jnp.where(keep_rows(), k.dvT[lanes, :].T[:ROWS] + k.tmp2[:, lanes], 0.0).astype(BF16)
    k.dpacked[:, lanes] = dq
    k.dpacked[:, slice(D + half * 128, D + half * 128 + 128)] = dk
    k.dpacked[:, slice(2 * D + half * 128, 2 * D + half * 128 + 128)] = dv
    k.store("qkv%d" % half, l, tn(k.a_normed[l], jnp.concatenate([dq, dk, dv], 1)))


def attn_bwd_end(l, k):
    g = k.g[...]
    dn = nt(k.dpacked[...], k.qkv[l]).astype(BF16).astype(F32)
    dx = norm_bwd(
        dn,
        k.a_xhat[l],
        k.a_rstd[l],
        k.againf[pl.ds(l, 1), :],
        lambda v: k.store_row("again", l, 0, slice(None), v),
        lambda v: k.store_row("abias", l, 0, slice(None), v),
    )
    dmixed = dx + g
    k.tmp[...] = dmixed
    conv_taps_grad(k.sx.at[l], k.tmp, 3, lambda tap, lanes, v: k.store_row("pos", l, tap, lanes, v))


def attn_bwd_input(l, k):
    dmixed = k.tmp[...]
    shifted_into(k.sd, dmixed, 3)
    conv_from(k.sd, k.posf.at[l], 3, True, k.tmp, k.tmp2)
    k.g[...] = jnp.where(keep_rows(), k.tmp2[...], 0.0).astype(BF16).astype(F32)


def prepare(k, tok, cot, routes):
    t = iota((ROWS, TOKS), 0)
    spread = ((t >> 4) * SIDE + (t & 15) == iota((ROWS, TOKS), 1)) & valid(t)
    spread = spread.astype(F32).astype(BF16)
    k.x[...] = nn(spread, tok)
    k.g[...] = nn(spread, cot)
    t = iota((ROWS, 128), 0)
    reg = jnp.where(valid(t), region_of(t), REGIONS)
    k.ekey[...] = (reg == iota((ROWS, 128), 1)).astype(F32).astype(BF16)
    t = iota((128, FULL), 1)
    k.eqT[...] = ((region_of(t) == iota((128, FULL), 0)) & valid(t)).astype(F32).astype(BF16)
    place = iota((128, REGIONS), 0)
    k.open[...] = jnp.zeros_like(k.open)
    k.pb[:, ROWS:, :] = jnp.zeros((k.pb.shape[0], FULL - ROWS, FULL), BF16)
    k.ds[:, ROWS:, :] = jnp.zeros((2, FULL - ROWS, FULL), BF16)
    for ref in (k.sx, k.sv):
        for l in range(ref.shape[0]):
            for b in range(ref.shape[1]):
                ref[l, b, :32] = jnp.zeros((32, D), F32)
                ref[l, b, 32 + ROWS :] = jnp.zeros((32, D), F32)
    for b in range(5):
        k.sd[b, :32] = jnp.zeros((32, D), F32)
        k.sd[b, 32 + ROWS :] = jnp.zeros((32, D), F32)
    for lh in range(k.open.shape[0]):
        hit = None
        for j in range(TOPK):
            same = routes[lh // HEADS, lh % HEADS, pl.ds(j, 1), :] == place
            hit = same if hit is None else hit | same
        k.open[lh, :, :REGIONS] = jnp.where(hit, 0.0, BLOCKED).astype(BF16)
    k.againf[:k.again.shape[0], :] = k.again[...].astype(F32)
    k.abiasf[:k.abias.shape[0], :] = k.abias[...].astype(F32)
    k.mgainf[:k.mgain.shape[0], :] = k.mgain[...].astype(F32)
    k.mbiasf[:k.mbias.shape[0], :] = k.mbias[...].astype(F32)
    for tap in range(9):
        k.posf[:, tap, :] = k.pos[tap].astype(F32)
    for tap in range(25):
        k.lepef[:, tap, :] = k.lepe[tap].astype(F32)


def scratch(layers):
    one = pltpu.VMEM
    return dict(
        againf=one((8, D), F32),
        abiasf=one((8, D), F32),
        mgainf=one((8, D), F32),
        mbiasf=one((8, D), F32),
        posf=one((layers, 16, D), F32),
        lepef=one((layers, 32, D), F32),
        x=one((ROWS, D), F32),
        g=one((ROWS, D), F32),
        tmp=one((ROWS, D), F32),
        tmp2=one((ROWS, D), F32),
        sx=one((layers, 3, 64 + ROWS, D), F32),
        sv=one((layers, 5, 64 + ROWS, D), F32),
        sd=one((5, 64 + ROWS, D), F32),
        a_xhat=one((layers, ROWS, D), F32),
        a_rstd=one((layers, ROWS, 1), F32),
        a_normed=one((layers, ROWS, D), BF16),
        key=one((layers, ROWS, D), BF16),
        val=one((layers, ROWS, D), BF16),
        qT=one((layers, D, FULL), BF16),
        kT=one((layers, D, FULL), BF16),
        vT=one((layers, D, FULL), BF16),
        oT=one((D, FULL), F32),
        dcT=one((D, FULL), BF16),
        dqT=one((D, FULL), F32),
        dkT=one((D, FULL), F32),
        dvT=one((D, FULL), F32),
        dpacked=one((ROWS, 3 * D), BF16),
        p=one((layers * HEADS, ROWS, FULL), F32),
        pb=one((layers * HEADS, FULL, FULL), BF16),
        ds=one((2, FULL, FULL), BF16),
        open=one((layers * HEADS, 128, 128), BF16),
        ekey=one((ROWS, 128), BF16),
        eqT=one((128, FULL), BF16),
        ctx=one((layers, ROWS, D), BF16),
        m_xhat=one((layers, ROWS, D), F32),
        m_rstd=one((layers, ROWS, 1), F32),
        m_normed=one((layers, ROWS, D), BF16),
        act=one((layers, ROWS, 3 * D), BF16),
        slope=one((layers, ROWS, 3 * D), F32),
    )


class Group:
    def __init__(self, where, axis, stride, size):
        self.where, self.axis, self.stride, self.size = where, axis, stride, size
        self.index = (where[axis] // stride) % size

    def member(self, j):
        at = list(self.where)
        at[self.axis] = self.where[self.axis] + (j - self.index) * self.stride
        return tuple(at)

    def after(self, step):
        return lax.rem(self.index + step, self.size)


class Exchange:
    def __init__(self, mine, total, base, rows, groups, bufs, send, recv):
        self.mine, self.total, self.groups = mine, total, groups
        self.bufs, self.send, self.recv = bufs, send, recv
        self.base, self.rows = [base], [rows]
        for group, split in groups:
            size = self.rows[-1] // group.size if split else self.rows[-1]
            self.rows.append(size)
            self.base.append(self.base[-1] + group.index * size if split else self.base[-1])
        self.flight = None

    def part(self, stage, j):
        size = self.rows[stage + 1]
        return pl.ds(pl.multiple_of(self.base[stage] + j * size, 16), size)

    def own(self, stage):
        return pl.ds(pl.multiple_of(self.base[stage], 16), self.rows[stage])

    def copy(self, sem, src, dst, to):
        return pltpu.make_async_remote_copy(
            src_ref=src,
            dst_ref=dst,
            send_sem=self.send.at[sem],
            recv_sem=self.recv.at[sem],
            device_id=to,
            device_id_type=pl.DeviceIdType.MESH,
        )

    def go(self, stage):
        group, split = self.groups[stage]
        sem, buf = self.bufs[stage]
        self.flight = []
        if not split:
            buf[group.index] = self.mine[self.own(stage), :]
        for step in range(1, group.size):
            to = group.after(step)
            if split:
                src, dst = self.mine.at[self.part(stage, to), :], buf.at[step - 1]
            else:
                src, dst = self.mine.at[self.own(stage), :], buf.at[group.index]
            copy = self.copy(sem + step - 1, src, dst, group.member(to))
            copy.start()
            if not split:
                came = lax.rem(group.index + group.size - step, group.size)
                copy = (copy, self.copy(sem + step - 1, src, buf.at[came], group.member(to)))
            else:
                copy = (copy, copy)
            self.flight.append(copy)

    def add(self, stage):
        group, split = self.groups[stage]
        _, buf = self.bufs[stage]
        for out, into in self.flight:
            out.wait_send()
            into.wait_recv()
        mine = self.own(stage + 1)
        last = stage + 1 == len(self.groups)
        to = self.total if last else self.mine
        if split:
            total = self.mine[mine, :].astype(F32)
            for step in range(group.size - 1):
                total = total + buf[step].astype(F32)
        else:
            total = buf[0].astype(F32)
            for j in range(1, group.size):
                total = total + buf[j].astype(F32)
        to[mine, :] = total.astype(BF16)

    def back(self, stage):
        group, split = self.groups[stage]
        self.flight = []
        if not split:
            return
        sem = self.bufs[stage][0] + group.size - 1
        rows = self.part(stage, group.index)
        for step in range(1, group.size):
            copy = self.copy(sem + step - 1, self.total.at[rows, :], self.total.at[rows, :], group.member(group.after(step)))
            copy.start()
            came = self.part(stage, lax.rem(group.index + group.size - step, group.size))
            into = self.copy(sem + step - 1, self.total.at[came, :], self.total.at[came, :], group.member(group.after(step)))
            self.flight.append((copy, into))

    def arrived(self):
        for out, into in self.flight:
            out.wait_send()
            into.wait_recv()

    def steps(self):
        last = len(self.groups) - 1
        for stage in range(last + 1):
            self.go(stage)
            yield
            self.add(stage)
        for stage in range(last, -1, -1):
            if self.groups[stage][1]:
                self.back(stage)
                yield
                self.arrived()


def groups_of(where, sections, dps):
    core = Group(where, 1, 1, 2)
    plane = Group(where, 0, 1, sections)
    far = min(4, dps // 2)
    line = Group(where, 1, 2, far)
    rest = dps // 2 // far
    more = [(Group(where, 1, 2 * far, rest), False)] if rest > 1 else []
    return core, plane, line, more


IN_NAMES = ("tok", "routes", "pos", "again", "abias", "qkv", "lepe", "proj", "mgain", "mbias", "fc1", "fc2", "cot")
G_NAMES = ("pos", "again", "abias", "qkv", "lepe", "proj", "mgain", "mbias", "fc1", "fc2")

SMALL = 128
LAST = 16


def row_map(layers):
    at, pieces, n = {}, [], 0
    for l in reversed(range(layers)):
        at["fc2", l], at["fc1", l] = n, n + 3 * D
        pieces.append((n, 6 * D))
        n += 6 * D
        start = n
        at["proj", l], at["qkv0", l] = n, n + D
        n += D + 384
        if l == 0:
            at["small"] = n
            n += SMALL
            pieces.append((start, n - start))
            start = n
        at["qkv1", l] = n
        n += 384
        pieces.append((start, n - start))
    at["last"] = n
    pieces.append((n, LAST))
    return at, pieces, n + LAST


def small_map(layers):
    at, n = {}, 0
    for l in reversed(range(layers)):
        names = (("pos", 9), ("again", 1), ("abias", 1), ("lepe", 25), ("mgain", 1), ("mbias", 1))
        for name, rows in names:
            if l == 0 and name in ("pos", "again", "abias"):
                continue
            at[name, l] = n
            n += rows
    assert n <= SMALL
    last = {("pos", 0): 0, ("again", 0): 9, ("abias", 0): 10}
    return at, last


def plan(where, sections, dps, layers):
    core, plane, line, more = groups_of(where, sections, dps)
    _, pieces, _ = row_map(layers)
    plans = []
    for n, (base, rows) in enumerate(pieces):
        shares = rows // 16
        groups = []
        for group in (core, plane, line):
            split = shares % group.size == 0
            if split:
                shares //= group.size
            groups.append((group, split))
        plans.append((base, rows, groups + more))
    return plans


def plan_buffers(plans):
    shapes, sems = [], 0
    where = []
    for base, rows, groups in plans:
        mine = []
        for group, split in groups:
            if split:
                rows //= group.size
                shapes.append(pltpu.VMEM((group.size - 1, rows, D), BF16))
                mine.append((sems, len(shapes) - 1))
                sems += 2 * (group.size - 1)
            else:
                shapes.append(pltpu.VMEM((group.size, rows, D), BF16))
                mine.append((sems, len(shapes) - 1))
                sems += group.size - 1
        where.append(mine)
    return shapes, sems, where


def body(layers, sections, dps, names, *refs):
    k = K()
    n_in = len(IN_NAMES)
    for name, ref in zip(IN_NAMES, refs[:n_in]):
        setattr(k, name, ref)
    out_ref, gin_ref, total = refs[n_in : n_in + 3]
    refs = refs[n_in + 3 :]
    for name, ref in zip(names, refs):
        setattr(k, name, ref)
    mine, small, last, send, recv = refs[len(names) : len(names) + 5]
    bufs = refs[len(names) + 5 :]

    where = (lax.axis_index("section"), lax.axis_index("dp"))
    plans = plan(where, sections, dps, layers)
    _, _, slots = plan_buffers(plans)
    barrier = pltpu.get_barrier_semaphore()
    partners = 0
    for group, _ in plans[0][2]:
        for step in range(1, group.size):
            pl.semaphore_signal(barrier, inc=1, device_id=group.member(group.after(step)), device_id_type=pl.DeviceIdType.MESH)
            partners += 1

    at, pieces, _ = row_map(layers)
    small_at, last_at = small_map(layers)

    def store(name, l, v):
        n = at[name, l]
        v = v.astype(BF16)
        if name == "fc1":
            for c in range(3):
                mine[pl.ds(n + c * D, D), :] = v[:, c * D : (c + 1) * D]
        elif name.startswith("qkv"):
            mine[pl.ds(n, D), :] = v[:, :D]
            mine[pl.ds(n + D, 128), :128] = v[:128, D:]
            mine[pl.ds(n + D, 128), 128:] = v[128:, D:]
        else:
            mine[pl.ds(n, v.shape[0]), :] = v

    def store_row(name, l, tap, lanes, v):
        if (name, l) in small_at:
            small[pl.ds(small_at[name, l] + tap, 1), lanes] = v
        else:
            last[pl.ds(last_at[name, l] + tap, 1), lanes] = v

    k.store = store
    k.store_row = store_row
    small[...] = jnp.zeros_like(small)
    last[...] = jnp.zeros_like(last)
    prepare(k, k.tok[0, 0], k.cot[0, 0], k.routes.at[0, 0])

    def fwd(l, carry):
        attn_fwd(l, k)
        mlp_fwd(l, k)
        return carry

    lax.fori_loop(0, layers, fwd, 0)
    t = iota((TOKS, ROWS), 1)
    gathered = ((t >> 4) * SIDE + (t & 15) == iota((TOKS, ROWS), 0)) & valid(t)
    gathered = gathered.astype(F32).astype(BF16)
    out_ref[0, 0] = nn(gathered, k.x[...].astype(BF16)).astype(BF16)

    moves = []
    for (base, rows, groups), slot in zip(plans, slots):
        moves.append(
            Exchange(mine, total, base, rows, groups, [(sem, bufs[n]) for sem, n in slot], send, recv).steps()
        )

    def step(n):
        next(moves[n], None)

    for i in range(layers):
        l = layers - 1 - i
        first = i == 0
        mlp_bwd(l, k)
        if first:
            pl.semaphore_wait(barrier, partners)
            step(0)
            attn_bwd_start(l, k)
            step(0)
            attn_bwd_lepe(l, k)
            attn_bwd_conv(l, k)
            attn_bwd_heads(l, k, 0)
            attn_bwd_heads(l, k, 1)
            step(1)
            attn_bwd_end(l, k)
            step(1)
            attn_bwd_input(l, k)
            step(0)
        else:
            step(2)
            attn_bwd_start(l, k)
            step(2)
            step(1)
            attn_bwd_lepe(l, k)
            small_rows = pl.ds(at["small"], SMALL)
            mine[small_rows, :] = small[...].astype(BF16)
            attn_bwd_conv(l, k)
            step(0)
            attn_bwd_heads(l, k, 0)
            step(3)
            step(1)
            attn_bwd_heads(l, k, 1)
            step(4)
            step(3)
            step(0)
            step(2)
            attn_bwd_end(l, k)
            mine[pl.ds(at["last"], LAST), :] = last[...].astype(BF16)
            step(5)
            step(4)
            step(1)
            attn_bwd_input(l, k)
    gin_ref[0, 0] = nn(gathered, k.g[...].astype(BF16)).astype(BF16)
    live = list(moves)
    while live:
        for m in list(live):
            if next(m, live) is live:
                live.remove(m)


def finish_body(layers, total, out_in, gin_in, out, gin, pos, again, abias, qkv, lepe, proj, mgain, mbias, fc1, fc2):
    at, _, _ = row_map(layers)
    small_at, last_at = small_map(layers)
    out[...] = out_in[...]
    gin[...] = gin_in[...]
    small = total[pl.ds(at["small"], SMALL), :].astype(F32)
    last = total[pl.ds(at["last"], LAST), :].astype(F32)

    def rows_of(name, l, count):
        if (name, l) in small_at:
            n = small_at[name, l]
            return small[n : n + count]
        n = last_at[name, l]
        return last[n : n + count]

    for l in range(layers):
        for name, ref, count in (("pos", pos, 9), ("lepe", lepe, 25)):
            rows = rows_of(name, l, count)
            for tap in range(count):
                ref[tap, pl.ds(l, 1), :] = rows[tap : tap + 1]
        for name, ref in (("again", again), ("abias", abias), ("mgain", mgain), ("mbias", mbias)):
            ref[pl.ds(l, 1), :] = rows_of(name, l, 1)
        n = at["fc2", l]
        fc2[l] = total[pl.ds(n, 3 * D), :].astype(F32)
        n = at["fc1", l]
        for c in range(3):
            fc1[l, :, c * D : (c + 1) * D] = total[pl.ds(n + c * D, D), :].astype(F32)
        n = at["proj", l]
        proj[l] = total[pl.ds(n, D), :].astype(F32)
        for half in range(2):
            n = at["qkv%d" % half, l]
            both = total[pl.ds(n, D), :].astype(F32)
            lo = half * 128
            qkv[l, :, lo : lo + 128] = both[:, :128]
            qkv[l, :, D + lo : D + lo + 128] = both[:, 128:]
            tail = total[pl.ds(n + D, 128), :].astype(F32)
            qkv[l, :128, 2 * D + lo : 2 * D + lo + 128] = tail[:, :128]
            qkv[l, 128:, 2 * D + lo : 2 * D + lo + 128] = tail[:, 128:]


def per_device(sections, dps, tokens, routes, pos, again, abias, qkv, lepe, proj, mgain, mbias, fc1, fc2, cot):
    layers = pos.shape[0]
    assert tokens.shape == (1, 1, TOKS, D)
    sc = scratch(layers)
    pos_t, lepe_t = (jnp.transpose(a, (1, 0, 2)) for a in (pos, lepe))
    routes_t = jnp.swapaxes(routes, -1, -2)
    args = (tokens, routes_t, pos_t, again, abias, qkv, lepe_t, proj, mgain, mbias, fc1, fc2, cot)
    vm = pl.BlockSpec(memory_space=pltpu.VMEM)
    _, _, count = row_map(layers)
    shapes, sems, _ = plan_buffers(plan((0, 0), sections, dps, layers))
    params = pltpu.CompilerParams(vmem_limit_bytes=60 * 2**20, collective_id=0, has_side_effects=True)
    out, gin, total = pl.pallas_call(
        partial(body, layers, sections, dps, tuple(sc)),
        out_shape=[jax.ShapeDtypeStruct(tokens.shape, BF16)] * 2 + [jax.ShapeDtypeStruct((count, D), BF16)],
        in_specs=[vm] * len(args),
        out_specs=[vm] * 3,
        scratch_shapes=list(sc.values())
        + [
            pltpu.VMEM((count, D), BF16),
            pltpu.VMEM((SMALL, D), F32),
            pltpu.VMEM((LAST, D), F32),
            pltpu.SemaphoreType.DMA((sems,)),
            pltpu.SemaphoreType.DMA((sems,)),
        ]
        + shapes,
        compiler_params=params,
        name="blocks",
    )(*args)
    weights = (pos_t, again, abias, qkv, lepe_t, proj, mgain, mbias, fc1, fc2)
    res = pl.pallas_call(
        partial(finish_body, layers),
        out_shape=[jax.ShapeDtypeStruct(tokens.shape, BF16)] * 2 + [jax.ShapeDtypeStruct(w.shape, F32) for w in weights],
        in_specs=[vm] * 3,
        out_specs=[vm] * 12,
        compiler_params=pltpu.CompilerParams(vmem_limit_bytes=40 * 2**20),
        name="widen",
    )(total, out, gin)
    res = list(res)
    res[2] = jnp.transpose(res[2], (1, 0, 2))
    res[6] = jnp.transpose(res[6], (1, 0, 2))
    return tuple(res)


def solution(mesh):
    image = P("section", "dp", None, None)
    sections, dps = mesh.shape["section"], mesh.shape["dp"]
    return jax.shard_map(
        partial(per_device, sections, dps),
        mesh=mesh,
        in_specs=(image, P("section", "dp", None, None, None, None)) + (P(),) * 10 + (image,),
        out_specs=(image, image) + (P(),) * 10,
        check_vma=False,
    )
```

time: 1280 us -> 67.9 us (0.05)
  waiting for transfers between devices: 366 us -> 0 us
  local copies, waits for them, and re-layouts: 264 us -> 3.54 us
  matrix products: 210 us -> 0 us
  other arithmetic: 180 us -> 0 us
  loops' own time: 167 us -> 0 us
  Pallas kernels: 0 us -> 63.4 us
  starting transfers between devices: 33.9 us -> 0 us
  blocking collectives: 30.9 us -> 0 us
  between operations: 15.9 us -> 0.67 us
    psum x3 -> x0, waiting for transfers between devices: 328 us -> none  [the longest x2 288 us: per_device(): summed = lax.psum(grad_sums, ('section', 'dp'))]
    another operation x14 -> x0, loops' own time: 167 us -> none  [the longest x7 153 us: per_device(): lax.switch(segment_index, backwards, saved_input, routed, incoming)]
    dot_general x133 -> x0, matrix products: 162 us -> none  [the longest x14 40.9 us: attn_pieces(): jnp.einsum('ihrqk,ihrkc->ihrqc', probs_low, picked_values, preferred_elem...]
    another operation x122 -> x0, local copies, waits for them, and re-layouts: 91.6 us -> none
    reshape x245 -> x0, local copies, waits for them, and re-layouts: 69.5 us -> none  [the longest x49 27.3 us: heads_of(): regional.reshape(images, region_count, inside, HEADS, channels // HEADS)]
    pallas_call x0 -> x2, Pallas kernels: none -> 63.4 us  [the longest x1 60.7 us: per_device(): pl.pallas_call(partial(body, layers, sections, dps, tuple(sc)), out_shape...]
    add x38 -> x0, other arithmetic: 59.7 us -> none  [the longest x28 51.6 us: depthwise(): summed + padded[:, row_tap:row_tap + SIDE, col_tap:col_tap + SIDE, :] * k...]
    sub x14 -> x0, matrix products: 48.3 us -> none  [attn_pieces(): attn_probs = jax.nn.softmax(scores, axis=-1)]
  transfers between devices with their start and end apart: 15 -> 0, of which waited for: 14 -> 0; matrix products, arithmetic and copies ran while one was open for 1% -> 0% of each run, Pallas kernels for 0% -> 0%
where the time goes in v1:
time: 67.9 us; the launch traced here: 67.6 us
  Pallas kernels  63.4 us (93%)
  local copies, waits for them, and re-layouts  3.54 us (5%)
    pallas_call x1, Pallas kernels, per_device(): pl.pallas_call(partial(body, layers, sections, dps, tuple(sc)), out_shape...  60.7 us
    unnamed x6, local copies, waits for them, and re-layouts  3.54 us
    pallas_call x1, Pallas kernels, per_device(): pl.pallas_call(partial(finish_body, layers), out_shape=[jax.ShapeDtypeStr...  2.7 us

profile of v1, /device:TPU:0, one launch (start us, length us, event | category | flops | bytes accessed | tf_op | source)
XLA Modules:
  0.0 67.6 jit_solution(11301725285710627838)
XLA Ops:
  0.6 60.7 %blocks.1 = (bf16[1,1,196,256]{3,2,1,0:T(8,128)(2,1)}, bf16[1,1,196,256]{3,2,1,0:T(8,128)(2,1)}, bf16[5264,256]{1,0:T(8,128)(2,1)}) custom-call(bf16[1,1,196,256]{3,2,1,0:T(8,128)(2,1)} %refs_0_.1, s32[1,1,2,8,4,49]{5,4,3,2,1,0:T(4,128)} %bitcast.5, bf16[9,2,256]{2,1,0:T(2,128)(2,1)} %bitcast.7, bf16[2,256]{1,0:T(2,128)(2,1)} %refs_3_.1, ...), custom_call_target="tpu_custom_call" | custom-call | tf_op jit(solution)/shard_map/blocks/pallas_call | solution.py:747
  61.4 0.0 copy-start
  61.4 1.8 %copy-done = bf16[5264,256]{1,0:T(8,128)(2,1)S(1)} copy-done((bf16[5264,256]{1,0:T(8,128)(2,1)S(1)}, bf16[5264,256]{1,0:T(8,128)(2,1)}, u32[]{:S(2)}) %copy-start) | copy-done | bytes 2695192
  63.1 0.0 copy-start.1
  63.1 0.9 %copy-done.1 = bf16[1,1,196,256]{3,2,1,0:T(8,128)(2,1)S(1)} copy-done((bf16[1,1,196,256]{3,2,1,0:T(8,128)(2,1)S(1)}, bf16[1,1,196,256]{3,2,1,0:T(8,128)(2,1)}, u32[]{:S(2)}) %copy-start.1) | copy-done | bytes 100376
  64.0 0.0 copy-start.2
  64.0 0.9 %copy-done.2 = bf16[1,1,196,256]{3,2,1,0:T(8,128)(2,1)S(1)} copy-done((bf16[1,1,196,256]{3,2,1,0:T(8,128)(2,1)S(1)}, bf16[1,1,196,256]{3,2,1,0:T(8,128)(2,1)}, u32[]{:S(2)}) %copy-start.2) | copy-done | bytes 100376
  64.9 2.7 %widen.1 = (bf16[1,1,196,256]{3,2,1,0:T(8,128)(2,1)}, bf16[1,1,196,256]{3,2,1,0:T(8,128)(2,1)}, f32[9,2,256]{2,1,0:T(2,128)}, f32[2,256]{1,0:T(2,128)}, f32[2,25...) custom-call(bf16[5264,256]{1,0:T(8,128)(2,1)S(1)} %copy-done, ...), custom_call_target="tpu_custom_call" | custom-call | tf_op jit(solution)/shard_map/widen/pallas_call | solution.py:765
Async XLA Ops:
  61.4 1.8 %copy-start = (bf16[5264,256]{1,0:T(8,128)(2,1)S(1)}, bf16[5264,256]{1,0:T(8,128)(2,1)}, u32[]{:S(2)}) copy-start(bf16[5264,256]{1,0:T(8,128)(2,1)} %get-tuple-element.27.total) | copy-start | bytes 8085508
  63.1 0.9 %copy-start.1 = (bf16[1,1,196,256]{3,2,1,0:T(8,128)(2,1)S(1)}, bf16[1,1,196,256]{3,2,1,0:T(8,128)(2,1)}, u32[]{:S(2)}) copy-start(bf16[1,1,196,256]{3,2,1,0:T(8,128)(2,1)} %get-tuple-element.28.out_in) | copy-start | bytes 301060
  64.0 0.9 %copy-start.2 = (bf16[1,1,196,256]{3,2,1,0:T(8,128)(2,1)S(1)}, bf16[1,1,196,256]{3,2,1,0:T(8,128)(2,1)}, u32[]{:S(2)}) copy-start(bf16[1,1,196,256]{3,2,1,0:T(8,128)(2,1)} %get-tuple-element.29.gin_in) | copy-start | bytes 301060

commit v2 on v1

--- a/solution.py
+++ b/solution.py
@@ -108,10 +108,13 @@
             store(tap, lanes, jnp.sum(s, axis=0, keepdims=True))
 
 
-def half_lanes_mask(h):
+def head_keys(half):
     lane = iota((1, 128), 1)
-    lo = (h % 4) * HD
-    return (lane >= lo) & (lane < lo + HD)
+    parts = []
+    for hh in range(4):
+        own = (lane >= hh * HD) & (lane < (hh + 1) * HD)
+        parts.append(jnp.where(own, half, jnp.zeros_like(half)))
+    return jnp.concatenate(parts, 0)
 
 
 def gelu_pair(x):
@@ -136,6 +139,7 @@
     bias = k.abiasf[pl.ds(l, 1), :]
     normed = jnp.where(keep_rows(), xhat * gain + bias, 0.0).astype(BF16)
     k.a_normed[l] = normed
+    k.need(l, "qkv")
     packed = nn(normed, k.qkv[l]).astype(BF16)
     q = packed[:, :D]
     key = packed[:, D : 2 * D]
@@ -143,33 +147,33 @@
     k.key[l] = key
     k.val[l] = val
     zpad = jnp.zeros((FULL - ROWS, D), BF16)
-    k.qT[l] = jnp.concatenate([q, zpad], 0).T
-    k.kT[l] = jnp.concatenate([key, zpad], 0).T
-    k.vT[l] = jnp.concatenate([val, zpad], 0).T
+    qT, kT, vT = (jnp.concatenate([part, zpad], 0).T for part in (q, key, val))
+    k.qT[l] = qT
+    k.kT[l] = kT
     shifted_into(k.sv.at[l], val.astype(F32), 5)
     conv_from(k.sv.at[l], k.lepef.at[l], 5, False, None, k.tmp2)
-    ekey = k.ekey[...]
     eqT = k.eqT[...]
     c = HD**-0.5 * LOG2E
+    zkeys = jnp.zeros((FULL - ROWS, FULL), BF16)
+    outs = []
     for half in range(2):
         lanes = slice(half * 128, half * 128 + 128)
-        rhs = jnp.concatenate([k.qT[l, lanes, :], eqT], 0)
-        khalf = k.key[l, :, lanes]
+        heads = pl.ds(l * HEADS + half * 4, 4)
+        rhs = jnp.concatenate([qT[lanes], eqT], 0)
+        lhs = jnp.concatenate([head_keys(key[:, lanes]), k.blocked[heads].reshape(4 * ROWS, 128)], 1)
+        s = nn(lhs, rhs).reshape(4, ROWS, FULL)
+        m = jnp.max(s, axis=1, keepdims=True)
+        e = jnp.exp2((s - m) * c)
+        p = e * (1.0 / jnp.sum(e, axis=1, keepdims=True))
+        k.p[heads] = p
+        pb = p.astype(BF16)
+        k.pb[heads, :ROWS] = pb
         for hh in range(4):
             h = half * 4 + hh
-            blocked = nn(ekey, k.open[l * HEADS + h]).astype(BF16)
-            lhs = jnp.concatenate([jnp.where(half_lanes_mask(h), khalf, jnp.zeros_like(khalf)), blocked], 1)
-            s = nn(lhs, rhs)
-            m = jnp.max(s, axis=0, keepdims=True)
-            e = jnp.exp2((s - m) * c)
-            r = 1.0 / jnp.sum(e, axis=0, keepdims=True)
-            p = e * r
-            k.p[l * HEADS + h] = p
-            pb = p.astype(BF16)
-            k.pb[l * HEADS + h, :ROWS] = pb
-            k.oT[pl.ds(h * HD, HD), :] = nn(k.vT[l, pl.ds(h * HD, HD), :], k.pb[l * HEADS + h])
-    ctx = (k.oT[...].T[:ROWS] + k.tmp2[...]).astype(BF16)
+            outs.append(nn(vT[h * HD : (h + 1) * HD], jnp.concatenate([pb[hh], zkeys], 0)))
+    ctx = (jnp.concatenate(outs, 0).T[:ROWS] + k.tmp2[...]).astype(BF16)
     k.ctx[l] = ctx
+    k.need(l, "proj")
     res = k.tmp[...] + nn(ctx, k.proj[l])
     k.x[...] = jnp.where(keep_rows(), res, 0.0).astype(BF16).astype(F32)
 
@@ -181,11 +185,13 @@
     k.m_rstd[l] = rstd
     normed = (xhat * k.mgainf[pl.ds(l, 1), :] + k.mbiasf[pl.ds(l, 1), :]).astype(BF16)
     k.m_normed[l] = normed
+    k.need(l, "fc1")
     hidden = nn(normed, k.fc1[l])
     act, slope = gelu_pair(hidden)
     act = act.astype(BF16)
     k.act[l] = act
     k.slope[l] = slope
+    k.need(l, "fc2")
     res = x + nn(act, k.fc2[l])
     k.x[...] = jnp.where(keep_rows(), res, 0.0).astype(BF16).astype(F32)
 
@@ -199,10 +205,13 @@
     return rstd * (dg - m1 - xhat * m2)
 
 
+def mlp_bwd_fc2(l, k):
+    k.store("fc2", l, tn(k.act[l], k.g[...].astype(BF16)))
+
+
 def mlp_bwd(l, k):
     g = k.g[...]
     gb = g.astype(BF16)
-    k.store("fc2", l, tn(k.act[l], gb))
     dact = nt(gb, k.fc2[l]).astype(BF16).astype(F32)
     dhid = (k.slope[l] * dact).astype(BF16)
     k.store("fc1", l, tn(k.m_normed[l], dhid))
@@ -224,14 +233,14 @@
     k.store("proj", l, tn(k.ctx[l], gb))
     dctx = nt(gb, k.proj[l]).astype(BF16)
     dctx32 = dctx.astype(F32)
-    k.tmp[...] = dctx32
+    k.dctx[l] = dctx32
     zpad = jnp.zeros((FULL - ROWS, D), BF16)
     k.dcT[...] = jnp.concatenate([dctx, zpad], 0).T
     shifted_into(k.sd, dctx32, 5)
 
 
 def attn_bwd_lepe(l, k):
-    conv_taps_grad(k.sv.at[l], k.tmp, 5, lambda tap, lanes, v: k.store_row("lepe", l, tap, lanes, v))
+    conv_taps_grad(k.sv.at[l], k.dctx.at[l], 5, lambda tap, lanes, v: k.store_row("lepe", l, tap, lanes, v))
 
 
 def attn_bwd_conv(l, k):
@@ -241,23 +250,26 @@
 def attn_bwd_heads(l, k, half):
     scale = HD**-0.5
     lanes = slice(half * 128, half * 128 + 128)
-    vhalf = k.val[l, :, lanes]
-    rhs = k.dcT[lanes, :]
+    heads = pl.ds(l * HEADS + half * 4, 4)
+    dcT = k.dcT[lanes]
+    qT, kT = k.qT[l, lanes], k.kT[l, lanes]
+    dp = nn(head_keys(k.val[l, :, lanes]), dcT).reshape(4, ROWS, FULL)
+    p = k.p[heads]
+    pb = k.pb[heads]
+    pd = p * dp
+    ds = (pd - p * jnp.sum(pd, axis=1, keepdims=True)).astype(BF16)
+    zkeys = jnp.zeros((FULL - ROWS, FULL), BF16)
+    dq, dk, dv = [], [], []
     for hh in range(4):
-        h = half * 4 + hh
-        hrows = pl.ds(h * HD, HD)
-        dp = nn(jnp.where(half_lanes_mask(h), vhalf, jnp.zeros_like(vhalf)), rhs)
-        k.dvT[hrows, :] = nt(k.dcT[hrows, :], k.pb[l * HEADS + h])
-        p = k.p[l * HEADS + h]
-        pd = p * dp
-        ds = pd - p * jnp.sum(pd, axis=0, keepdims=True)
-        k.ds[hh % 2, :ROWS] = ds.astype(BF16)
-        dsb = k.ds[hh % 2]
-        k.dqT[hrows, :] = nn(k.kT[l, hrows, :], dsb) * scale
-        k.dkT[hrows, :] = nt(k.qT[l, hrows, :], dsb) * scale
-    dq = k.dqT[lanes, :].T[:ROWS].astype(BF16)
-    dk = k.dkT[lanes, :].T[:ROWS].astype(BF16)
-    dv = jnp.where(keep_rows(), k.dvT[lanes, :].T[:ROWS] + k.tmp2[:, lanes], 0.0).astype(BF16)
+        rows = slice(hh * HD, (hh + 1) * HD)
+        dsb = jnp.concatenate([ds[hh], zkeys], 0)
+        dv.append(nt(dcT[rows], pb[hh]))
+        dq.append(nn(kT[rows], dsb))
+        dk.append(nt(qT[rows], dsb))
+    dq, dk, dv = (jnp.concatenate(part, 0).T[:ROWS] for part in (dq, dk, dv))
+    dq = (dq * scale).astype(BF16)
+    dk = (dk * scale).astype(BF16)
+    dv = jnp.where(keep_rows(), dv + k.tmp2[:, lanes], 0.0).astype(BF16)
     k.dpacked[:, lanes] = dq
     k.dpacked[:, slice(D + half * 128, D + half * 128 + 128)] = dk
     k.dpacked[:, slice(2 * D + half * 128, 2 * D + half * 128 + 128)] = dv
@@ -276,14 +288,16 @@
         lambda v: k.store_row("abias", l, 0, slice(None), v),
     )
     dmixed = dx + g
-    k.tmp[...] = dmixed
-    conv_taps_grad(k.sx.at[l], k.tmp, 3, lambda tap, lanes, v: k.store_row("pos", l, tap, lanes, v))
+    k.dmixed[l] = dmixed
+
+
+def attn_bwd_pos(l, k):
+    conv_taps_grad(k.sx.at[l], k.dmixed.at[l], 3, lambda tap, lanes, v: k.store_row("pos", l, tap, lanes, v))
 
 
 def attn_bwd_input(l, k):
-    dmixed = k.tmp[...]
-    shifted_into(k.sd, dmixed, 3)
-    conv_from(k.sd, k.posf.at[l], 3, True, k.tmp, k.tmp2)
+    shifted_into(k.sd, k.dmixed[l], 3)
+    conv_from(k.sd, k.posf.at[l], 3, True, k.dmixed.at[l], k.tmp2)
     k.g[...] = jnp.where(keep_rows(), k.tmp2[...], 0.0).astype(BF16).astype(F32)
 
 
@@ -301,7 +315,6 @@
     place = iota((128, REGIONS), 0)
     k.open[...] = jnp.zeros_like(k.open)
     k.pb[:, ROWS:, :] = jnp.zeros((k.pb.shape[0], FULL - ROWS, FULL), BF16)
-    k.ds[:, ROWS:, :] = jnp.zeros((2, FULL - ROWS, FULL), BF16)
     for ref in (k.sx, k.sv):
         for l in range(ref.shape[0]):
             for b in range(ref.shape[1]):
@@ -310,12 +323,17 @@
     for b in range(5):
         k.sd[b, :32] = jnp.zeros((32, D), F32)
         k.sd[b, 32 + ROWS :] = jnp.zeros((32, D), F32)
-    for lh in range(k.open.shape[0]):
+    ekey = k.ekey[...]
+    for lh in range(k.blocked.shape[0]):
         hit = None
         for j in range(TOPK):
             same = routes[lh // HEADS, lh % HEADS, pl.ds(j, 1), :] == place
             hit = same if hit is None else hit | same
         k.open[lh, :, :REGIONS] = jnp.where(hit, 0.0, BLOCKED).astype(BF16)
+    for lh in range(0, k.blocked.shape[0], 2):
+        both = nn(ekey, jnp.concatenate([k.open[lh], k.open[lh + 1]], 1)).astype(BF16)
+        k.blocked[lh] = both[:, :128]
+        k.blocked[lh + 1] = both[:, 128:]
     k.againf[:k.again.shape[0], :] = k.again[...].astype(F32)
     k.abiasf[:k.abias.shape[0], :] = k.abias[...].astype(F32)
     k.mgainf[:k.mgain.shape[0], :] = k.mgain[...].astype(F32)
@@ -349,16 +367,13 @@
         val=one((layers, ROWS, D), BF16),
         qT=one((layers, D, FULL), BF16),
         kT=one((layers, D, FULL), BF16),
-        vT=one((layers, D, FULL), BF16),
-        oT=one((D, FULL), F32),
         dcT=one((D, FULL), BF16),
-        dqT=one((D, FULL), F32),
-        dkT=one((D, FULL), F32),
-        dvT=one((D, FULL), F32),
         dpacked=one((ROWS, 3 * D), BF16),
+        dctx=one((layers, ROWS, D), F32),
+        dmixed=one((layers, ROWS, D), F32),
         p=one((layers * HEADS, ROWS, FULL), F32),
         pb=one((layers * HEADS, FULL, FULL), BF16),
-        ds=one((2, FULL, FULL), BF16),
+        blocked=one((layers * HEADS, ROWS, 128), BF16),
         open=one((layers * HEADS, 128, 128), BF16),
         ekey=one((ROWS, 128), BF16),
         eqT=one((128, FULL), BF16),
@@ -372,9 +387,9 @@
 
 
 class Group:
-    def __init__(self, where, axis, stride, size):
+    def __init__(self, where, axis, stride, size, index=None):
         self.where, self.axis, self.stride, self.size = where, axis, stride, size
-        self.index = (where[axis] // stride) % size
+        self.index = (where[axis] // stride) % size if index is None else index
 
     def member(self, j):
         at = list(self.where)
@@ -486,71 +501,85 @@
 
 
 def groups_of(where, sections, dps):
-    core = Group(where, 1, 1, 2)
-    plane = Group(where, 0, 1, sections)
-    far = min(4, dps // 2)
-    line = Group(where, 1, 2, far)
-    rest = dps // 2 // far
-    more = [(Group(where, 1, 2 * far, rest), False)] if rest > 1 else []
-    return core, plane, line, more
+    assert sections == 4 and dps % 8 == 0
+    core = where[1] % 2
+    low, high = where[0] % 2, where[0] // 2
+    return {
+        "c": Group(where, 1, 1, 2),
+        "x": Group(where, 0, 1, 2),
+        "y": Group(where, 0, 2, 2),
+        "p": Group(where, 0, 1, 4),
+        "u": Group(where, 0, 1 + core, 2, low + core * (high - low)),
+        "v": Group(where, 0, 2 - core, 2, high + core * (low - high)),
+        "z": Group(where, 1, 2, 2),
+        "w": Group(where, 1, 4, 2),
+        "q": Group(where, 1, 2, 4),
+        "r": Group(where, 1, 8, dps // 8),
+    }
 
 
 IN_NAMES = ("tok", "routes", "pos", "again", "abias", "qkv", "lepe", "proj", "mgain", "mbias", "fc1", "fc2", "cot")
 G_NAMES = ("pos", "again", "abias", "qkv", "lepe", "proj", "mgain", "mbias", "fc1", "fc2")
 
-SMALL = 128
-LAST = 16
+LAST = 80
+LANES = 128
+
+PIECES = (
+    (1536, "cpq"),
+    (1536, "cpq"),
+    (2048, "cpq"),
+    (1536, "cpq"),
+    (1536, "cpq"),
+    (512, "cpq"),
+    (1536, "cpq"),
+    (160, "cPQ"),
+)
+ORDER = (
+    "wait", "a1", 0, "b1", 1, "s1", 0, "c1", 1, "h1", "k1", 2, "e1", "i1", "a0", 2, 0, 3, "b0", 4, "s0",
+    3, 5, "c0", 1, 4, 5, "h0", 0, "k0", 2, 6, "e0", 1, "i0", "grad", 3, 6, "l1", "p1", "l0", "p0",
+    "last", "out", 0, 4, 5, 2, 7, 7, 1, 3, 6, 4, 2, 5, 0, 7, 3, 0, 6, 1, 4, 5, 1, 7, 2, 7, 6, 2, 3, 3, 4,
+    5, 4, 5, 6, 6,
+)
 
 
 def row_map(layers):
-    at, pieces, n = {}, [], 0
+    at, n = {}, 0
     for l in reversed(range(layers)):
-        at["fc2", l], at["fc1", l] = n, n + 3 * D
-        pieces.append((n, 6 * D))
-        n += 6 * D
-        start = n
-        at["proj", l], at["qkv0", l] = n, n + D
-        n += D + 384
-        if l == 0:
-            at["small"] = n
-            n += SMALL
-            pieces.append((start, n - start))
-            start = n
-        at["qkv1", l] = n
-        n += 384
-        pieces.append((start, n - start))
+        for name, rows in (("fc2", 6 * D), ("fc1", 6 * D), ("proj", 2 * D), ("qkv0", 3 * D), ("qkv1", 3 * D)):
+            at[name, l] = n
+            n += rows
     at["last"] = n
-    pieces.append((n, LAST))
-    return at, pieces, n + LAST
+    return at, n + 2 * LAST
 
 
 def small_map(layers):
     at, n = {}, 0
     for l in reversed(range(layers)):
-        names = (("pos", 9), ("again", 1), ("abias", 1), ("lepe", 25), ("mgain", 1), ("mbias", 1))
-        for name, rows in names:
-            if l == 0 and name in ("pos", "again", "abias"):
-                continue
+        for name, rows in (("pos", 9), ("again", 1), ("abias", 1), ("lepe", 25), ("mgain", 1), ("mbias", 1)):
             at[name, l] = n
             n += rows
-    assert n <= SMALL
-    last = {("pos", 0): 0, ("again", 0): 9, ("abias", 0): 10}
-    return at, last
+    assert n <= LAST
+    return at
+
+
+def pieces_of(layers):
+    assert layers == 2
+    pieces, n = [], 0
+    for rows, way in PIECES:
+        pieces.append((n, rows, way))
+        n += rows
+    assert n == row_map(layers)[1]
+    return pieces
 
 
 def plan(where, sections, dps, layers):
-    core, plane, line, more = groups_of(where, sections, dps)
-    _, pieces, _ = row_map(layers)
+    kinds = groups_of(where, sections, dps)
+    pieces = pieces_of(layers)
     plans = []
-    for n, (base, rows) in enumerate(pieces):
-        shares = rows // 16
-        groups = []
-        for group in (core, plane, line):
-            split = shares % group.size == 0
-            if split:
-                shares //= group.size
-            groups.append((group, split))
-        plans.append((base, rows, groups + more))
+    for base, rows, way in pieces:
+        if kinds["r"].size > 1:
+            way += "R"
+        plans.append((base, rows, [(kinds[letter.lower()], letter.islower()) for letter in way]))
     return plans
 
 
@@ -562,11 +591,11 @@
         for group, split in groups:
             if split:
                 rows //= group.size
-                shapes.append(pltpu.VMEM((group.size - 1, rows, D), BF16))
+                shapes.append(pltpu.VMEM((group.size - 1, rows, LANES), BF16))
                 mine.append((sems, len(shapes) - 1))
                 sems += 2 * (group.size - 1)
             else:
-                shapes.append(pltpu.VMEM((group.size, rows, D), BF16))
+                shapes.append(pltpu.VMEM((group.size, rows, LANES), BF16))
                 mine.append((sems, len(shapes) - 1))
                 sems += group.size - 1
         where.append(mine)
@@ -576,63 +605,70 @@
 def body(layers, sections, dps, names, *refs):
     k = K()
     n_in = len(IN_NAMES)
-    for name, ref in zip(IN_NAMES, refs[:n_in]):
-        setattr(k, name, ref)
+    given = dict(zip(IN_NAMES, refs[:n_in]))
     out_ref, gin_ref, total = refs[n_in : n_in + 3]
     refs = refs[n_in + 3 :]
     for name, ref in zip(names, refs):
         setattr(k, name, ref)
-    mine, small, last, send, recv = refs[len(names) : len(names) + 5]
-    bufs = refs[len(names) + 5 :]
+    refs = refs[len(names) :]
+    load = refs[n_in]
+    loads = {}
+    for i, name in enumerate(IN_NAMES):
+        setattr(k, name, refs[i])
+        loads[name] = pltpu.make_async_copy(given[name], refs[i], load.at[i])
+    for name in LOAD_ORDER:
+        loads[name].start()
+    mine, last, send, recv = refs[n_in + 1 : n_in + 5]
+    bufs = refs[n_in + 5 :]
 
     where = (lax.axis_index("section"), lax.axis_index("dp"))
     plans = plan(where, sections, dps, layers)
     _, _, slots = plan_buffers(plans)
     barrier = pltpu.get_barrier_semaphore()
     partners = 0
-    for group, _ in plans[0][2]:
+    kinds = groups_of(where, sections, dps)
+    for kind in "cpqr":
+        group = kinds[kind]
         for step in range(1, group.size):
             pl.semaphore_signal(barrier, inc=1, device_id=group.member(group.after(step)), device_id_type=pl.DeviceIdType.MESH)
             partners += 1
 
-    at, pieces, _ = row_map(layers)
-    small_at, last_at = small_map(layers)
+    at, _ = row_map(layers)
+    small_at = small_map(layers)
+
+    def need(l, name):
+        if l == 0:
+            loads[name].wait()
 
     def store(name, l, v):
         n = at[name, l]
         v = v.astype(BF16)
-        if name == "fc1":
-            for c in range(3):
-                mine[pl.ds(n + c * D, D), :] = v[:, c * D : (c + 1) * D]
-        elif name.startswith("qkv"):
-            mine[pl.ds(n, D), :] = v[:, :D]
-            mine[pl.ds(n + D, 128), :128] = v[:128, D:]
-            mine[pl.ds(n + D, 128), 128:] = v[128:, D:]
-        else:
-            mine[pl.ds(n, v.shape[0]), :] = v
+        height = v.shape[0]
+        for c in range(v.shape[1] // LANES):
+            mine[pl.ds(n + c * height, height), :] = v[:, c * LANES : (c + 1) * LANES]
 
     def store_row(name, l, tap, lanes, v):
-        if (name, l) in small_at:
-            small[pl.ds(small_at[name, l] + tap, 1), lanes] = v
-        else:
-            last[pl.ds(last_at[name, l] + tap, 1), lanes] = v
-
+        last[pl.ds(small_at[name, l] + tap, 1), lanes] = v
+
+    def flush(ref, n):
+        for c in range(2):
+            mine[pl.ds(n + c * ref.shape[0], ref.shape[0]), :] = ref[:, c * LANES : (c + 1) * LANES].astype(BF16)
+
+    k.need = need
     k.store = store
     k.store_row = store_row
-    small[...] = jnp.zeros_like(small)
     last[...] = jnp.zeros_like(last)
+    for name in LOAD_ORDER:
+        if name not in LATE:
+            loads[name].wait()
     prepare(k, k.tok[0, 0], k.cot[0, 0], k.routes.at[0, 0])
 
-    def fwd(l, carry):
+    for l in range(layers):
         attn_fwd(l, k)
         mlp_fwd(l, k)
-        return carry
-
-    lax.fori_loop(0, layers, fwd, 0)
     t = iota((TOKS, ROWS), 1)
     gathered = ((t >> 4) * SIDE + (t & 15) == iota((TOKS, ROWS), 0)) & valid(t)
     gathered = gathered.astype(F32).astype(BF16)
-    out_ref[0, 0] = nn(gathered, k.x[...].astype(BF16)).astype(BF16)
 
     moves = []
     for (base, rows, groups), slot in zip(plans, slots):
@@ -640,52 +676,37 @@
             Exchange(mine, total, base, rows, groups, [(sem, bufs[n]) for sem, n in slot], send, recv).steps()
         )
 
-    def step(n):
-        next(moves[n], None)
-
-    for i in range(layers):
-        l = layers - 1 - i
-        first = i == 0
-        mlp_bwd(l, k)
-        if first:
-            pl.semaphore_wait(barrier, partners)
-            step(0)
-            attn_bwd_start(l, k)
-            step(0)
-            attn_bwd_lepe(l, k)
-            attn_bwd_conv(l, k)
-            attn_bwd_heads(l, k, 0)
-            attn_bwd_heads(l, k, 1)
-            step(1)
-            attn_bwd_end(l, k)
-            step(1)
-            attn_bwd_input(l, k)
-            step(0)
+    def finish_out():
+        out_ref[0, 0] = nn(gathered, k.x[...].astype(BF16)).astype(BF16)
+
+    def finish_grad():
+        gin_ref[0, 0] = nn(gathered, k.g[...].astype(BF16)).astype(BF16)
+
+    work = {
+        "wait": lambda: pl.semaphore_wait(barrier, partners),
+        "out": finish_out,
+        "grad": finish_grad,
+        "last": lambda: flush(last, at["last"]),
+    }
+    for l in range(layers):
+        for name, run in (
+            ("a", mlp_bwd_fc2),
+            ("b", mlp_bwd),
+            ("s", attn_bwd_start),
+            ("l", attn_bwd_lepe),
+            ("c", attn_bwd_conv),
+            ("h", partial(attn_bwd_heads, half=0)),
+            ("k", partial(attn_bwd_heads, half=1)),
+            ("e", attn_bwd_end),
+            ("i", attn_bwd_input),
+            ("p", attn_bwd_pos),
+        ):
+            work[name + str(l)] = partial(run, l, k)
+    for item in ORDER:
+        if item in work:
+            work[item]()
         else:
-            step(2)
-            attn_bwd_start(l, k)
-            step(2)
-            step(1)
-            attn_bwd_lepe(l, k)
-            small_rows = pl.ds(at["small"], SMALL)
-            mine[small_rows, :] = small[...].astype(BF16)
-            attn_bwd_conv(l, k)
-            step(0)
-            attn_bwd_heads(l, k, 0)
-            step(3)
-            step(1)
-            attn_bwd_heads(l, k, 1)
-            step(4)
-            step(3)
-            step(0)
-            step(2)
-            attn_bwd_end(l, k)
-            mine[pl.ds(at["last"], LAST), :] = last[...].astype(BF16)
-            step(5)
-            step(4)
-            step(1)
-            attn_bwd_input(l, k)
-    gin_ref[0, 0] = nn(gathered, k.g[...].astype(BF16)).astype(BF16)
+            next(moves[item], None)
     live = list(moves)
     while live:
         for m in list(live):
@@ -693,44 +714,57 @@
                 live.remove(m)
 
 
-def finish_body(layers, total, out_in, gin_in, out, gin, pos, again, abias, qkv, lepe, proj, mgain, mbias, fc1, fc2):
-    at, _, _ = row_map(layers)
-    small_at, last_at = small_map(layers)
-    out[...] = out_in[...]
-    gin[...] = gin_in[...]
-    small = total[pl.ds(at["small"], SMALL), :].astype(F32)
-    last = total[pl.ds(at["last"], LAST), :].astype(F32)
-
-    def rows_of(name, l, count):
-        if (name, l) in small_at:
+def finish_body(layers, total, out_in, gin_in, *refs):
+    outs = refs[:12]
+    made = refs[12:24]
+    sems = refs[24]
+    at, _ = row_map(layers)
+    small_at = small_map(layers)
+    copies = []
+
+    def go(src, dst):
+        copy = pltpu.make_async_copy(src, dst, sems.at[len(copies)])
+        copy.start()
+        copies.append(copy)
+
+    go(out_in, outs[0])
+    go(gin_in, outs[1])
+    places = dict(zip(G_NAMES, range(2, 12)))
+
+    def wide(name, l, parts):
+        ref = made[places[name]]
+        for n, rows, top, col in parts:
+            ref[l, pl.ds(top, rows), pl.ds(col, LANES)] = total[pl.ds(n, rows), :].astype(F32)
+        go(ref.at[l], outs[places[name]].at[l])
+
+    for l in reversed(range(layers)):
+        wide("fc2", l, [(at["fc2", l] + c * 3 * D, 3 * D, 0, c * LANES) for c in range(2)])
+        wide("fc1", l, [(at["fc1", l] + c * D, D, 0, c * LANES) for c in range(6)])
+        wide("proj", l, [(at["proj", l] + c * D, D, 0, c * LANES) for c in range(2)])
+        wide("qkv", l, [(at["qkv%d" % h, l] + c * D, D, 0, c * D + h * LANES) for c in range(3) for h in range(2)])
+
+    def rows_from(n, count):
+        return [total[pl.ds(n + c * count, count), :].astype(F32) for c in range(2)]
+
+    both = rows_from(at["last"], LAST)
+    for name, count in (("pos", 9), ("lepe", 25), ("again", 1), ("abias", 1), ("mgain", 1), ("mbias", 1)):
+        ref = made[places[name]]
+        for l in range(layers):
             n = small_at[name, l]
-            return small[n : n + count]
-        n = last_at[name, l]
-        return last[n : n + count]
-
-    for l in range(layers):
-        for name, ref, count in (("pos", pos, 9), ("lepe", lepe, 25)):
-            rows = rows_of(name, l, count)
-            for tap in range(count):
-                ref[tap, pl.ds(l, 1), :] = rows[tap : tap + 1]
-        for name, ref in (("again", again), ("abias", abias), ("mgain", mgain), ("mbias", mbias)):
-            ref[pl.ds(l, 1), :] = rows_of(name, l, 1)
-        n = at["fc2", l]
-        fc2[l] = total[pl.ds(n, 3 * D), :].astype(F32)
-        n = at["fc1", l]
-        for c in range(3):
-            fc1[l, :, c * D : (c + 1) * D] = total[pl.ds(n + c * D, D), :].astype(F32)
-        n = at["proj", l]
-        proj[l] = total[pl.ds(n, D), :].astype(F32)
-        for half in range(2):
-            n = at["qkv%d" % half, l]
-            both = total[pl.ds(n, D), :].astype(F32)
-            lo = half * 128
-            qkv[l, :, lo : lo + 128] = both[:, :128]
-            qkv[l, :, D + lo : D + lo + 128] = both[:, 128:]
-            tail = total[pl.ds(n + D, 128), :].astype(F32)
-            qkv[l, :128, 2 * D + lo : 2 * D + lo + 128] = tail[:, :128]
-            qkv[l, 128:, 2 * D + lo : 2 * D + lo + 128] = tail[:, 128:]
+            for c in range(2):
+                lanes = pl.ds(c * LANES, LANES)
+                if count == 1:
+                    ref[pl.ds(l, 1), lanes] = both[c][n : n + 1]
+                else:
+                    for tap in range(count):
+                        ref[tap, pl.ds(l, 1), lanes] = both[c][n + tap : n + tap + 1]
+        go(ref, outs[places[name]])
+    for copy in copies:
+        copy.wait()
+
+
+LOAD_ORDER = ("tok", "routes", "cot", "pos", "again", "abias", "lepe", "mgain", "mbias", "qkv", "proj", "fc1", "fc2")
+LATE = ("qkv", "proj", "fc1", "fc2")
 
 
 def per_device(sections, dps, tokens, routes, pos, again, abias, qkv, lepe, proj, mgain, mbias, fc1, fc2, cot):
@@ -741,18 +775,20 @@
     routes_t = jnp.swapaxes(routes, -1, -2)
     args = (tokens, routes_t, pos_t, again, abias, qkv, lepe_t, proj, mgain, mbias, fc1, fc2, cot)
     vm = pl.BlockSpec(memory_space=pltpu.VMEM)
-    _, _, count = row_map(layers)
+    hbm = pl.BlockSpec(memory_space=pl.ANY)
+    _, count = row_map(layers)
     shapes, sems, _ = plan_buffers(plan((0, 0), sections, dps, layers))
-    params = pltpu.CompilerParams(vmem_limit_bytes=60 * 2**20, collective_id=0, has_side_effects=True)
+    params = pltpu.CompilerParams(vmem_limit_bytes=58 * 2**20, collective_id=0, has_side_effects=True)
     out, gin, total = pl.pallas_call(
         partial(body, layers, sections, dps, tuple(sc)),
-        out_shape=[jax.ShapeDtypeStruct(tokens.shape, BF16)] * 2 + [jax.ShapeDtypeStruct((count, D), BF16)],
-        in_specs=[vm] * len(args),
+        out_shape=[pltpu.VMEM(tokens.shape, BF16)] * 2 + [pltpu.VMEM((count, LANES), BF16)],
+        in_specs=[hbm] * len(args),
         out_specs=[vm] * 3,
         scratch_shapes=list(sc.values())
+        + [pltpu.VMEM(a.shape, a.dtype) for a in args]
         + [
-            pltpu.VMEM((count, D), BF16),
-            pltpu.VMEM((SMALL, D), F32),
+            pltpu.SemaphoreType.DMA((len(args),)),
+            pltpu.VMEM((count, LANES), BF16),
             pltpu.VMEM((LAST, D), F32),
             pltpu.SemaphoreType.DMA((sems,)),
             pltpu.SemaphoreType.DMA((sems,)),
@@ -762,12 +798,14 @@
         name="blocks",
     )(*args)
     weights = (pos_t, again, abias, qkv, lepe_t, proj, mgain, mbias, fc1, fc2)
+    shapes = [jax.ShapeDtypeStruct(tokens.shape, BF16)] * 2 + [jax.ShapeDtypeStruct(w.shape, F32) for w in weights]
     res = pl.pallas_call(
         partial(finish_body, layers),
-        out_shape=[jax.ShapeDtypeStruct(tokens.shape, BF16)] * 2 + [jax.ShapeDtypeStruct(w.shape, F32) for w in weights],
+        out_shape=shapes,
         in_specs=[vm] * 3,
-        out_specs=[vm] * 12,
-        compiler_params=pltpu.CompilerParams(vmem_limit_bytes=40 * 2**20),
+        out_specs=[hbm] * 12,
+        scratch_shapes=[pltpu.VMEM(a.shape, a.dtype) for a in shapes] + [pltpu.SemaphoreType.DMA((2 + 4 * layers + 6,))],
+        compiler_params=pltpu.CompilerParams(vmem_limit_bytes=32 * 2**20),
         name="widen",
     )(total, out, gin)
     res = list(res)

time: 67.9 us -> 50.7 us (0.75)
  Pallas kernels: 63.4 us -> 49.7 us
  local copies, waits for them, and re-layouts: 3.54 us -> 0 us
    pallas_call x1, Pallas kernels: 60.7 us -> 47.1 us  [per_device(): pl.pallas_call(partial(body, layers, sections, dps, tuple(sc)), out_shape...]
    unnamed x6 -> x0, local copies, waits for them, and re-layouts: 3.54 us -> none
where the time goes in v2:
time: 50.7 us; the launch traced here: 50.5 us
  Pallas kernels  49.7 us (98%)
  between operations  0.82 us (2%)
    pallas_call x1, Pallas kernels, per_device(): pl.pallas_call(partial(body, layers, sections, dps, tuple(sc)), out_shape...  47.1 us
    pallas_call x1, Pallas kernels, per_device(): pl.pallas_call(partial(finish_body, layers), out_shape=shapes, in_specs=[...  2.56 us

profile of v2, /device:TPU:0, one launch (start us, length us, event | category | flops | bytes accessed | tf_op | source)
XLA Modules:
  0.0 50.5 jit_solution(11969617617585639770)
XLA Ops:
  0.6 47.1 %blocks.1 = (bf16[1,1,196,256]{3,2,1,0:T(8,128)(2,1)S(1)}, bf16[1,1,196,256]{3,2,1,0:T(8,128)(2,1)S(1)}, bf16[10400,128]{1,0:T(8,128)(2,1)S(1)}) custom-call(bf16[1,1,196,256]{3,2,1,0:T(8,128)(2,1)} %refs_0_.1, s32[1,1,2,8,4,49]{5,4,3,2,1,0:T(4,128)} %bitcast.5, bf16[9,2,256]{2,1,0:T(2,128)(2,1)} %bitcast.7, bf16[2,256]{1,0:T(2,128)(2,1)} %refs_3_.1, ...), custom_call_target="tpu_custom_call" | custom-call | tf_op jit(solution)/shard_map/blocks/pallas_call | solution.py:782
  47.8 2.6 %widen.1 = (bf16[1,1,196,256]{3,2,1,0:T(8,128)(2,1)}, bf16[1,1,196,256]{3,2,1,0:T(8,128)(2,1)}, f32[9,2,256]{2,1,0:T(2,128)}, f32[2,256]{1,0:T(2,128)}, f32[2,25...) custom-call(bf16[10400,128]{1,0:T(8,128)(2,1)S(1)} %get-tuple-elemen, ...), custom_call_target="tpu_custom_call" | custom-call | tf_op jit(solution)/shard_map/widen/pallas_call | solution.py:802

commit v3 on v2

--- a/solution.py
+++ b/solution.py
@@ -409,7 +409,7 @@
             size = self.rows[-1] // group.size if split else self.rows[-1]
             self.rows.append(size)
             self.base.append(self.base[-1] + group.index * size if split else self.base[-1])
-        self.flight = None
+        self.flight, self.owed = None, []
 
     def part(self, stage, j):
         size = self.rows[stage + 1]
@@ -428,10 +428,14 @@
             device_id_type=pl.DeviceIdType.MESH,
         )
 
+    def started(self, sem, like):
+        self.flight = self.copy(sem, like, like, self.groups[0][0].member(self.groups[0][0].after(1)))
+        self.owed.append(self.flight)
+
     def go(self, stage):
         group, split = self.groups[stage]
         sem, buf = self.bufs[stage]
-        self.flight = []
+        others = group.size - 1
         if not split:
             buf[group.index] = self.mine[self.own(stage), :]
         for step in range(1, group.size):
@@ -440,21 +444,15 @@
                 src, dst = self.mine.at[self.part(stage, to), :], buf.at[step - 1]
             else:
                 src, dst = self.mine.at[self.own(stage), :], buf.at[group.index]
-            copy = self.copy(sem + step - 1, src, dst, group.member(to))
-            copy.start()
-            if not split:
-                came = lax.rem(group.index + group.size - step, group.size)
-                copy = (copy, self.copy(sem + step - 1, src, buf.at[came], group.member(to)))
-            else:
-                copy = (copy, copy)
-            self.flight.append(copy)
+            self.copy(sem, src, dst, group.member(to)).start()
+        self.started(sem, buf if split else buf.at[pl.ds(0, others)])
 
     def add(self, stage):
         group, split = self.groups[stage]
         _, buf = self.bufs[stage]
-        for out, into in self.flight:
-            out.wait_send()
-            into.wait_recv()
+        if not split:
+            self.owed.pop().wait_send()
+        self.flight.wait_recv()
         mine = self.own(stage + 1)
         last = stage + 1 == len(self.groups)
         to = self.total if last else self.mine
@@ -469,23 +467,13 @@
         to[mine, :] = total.astype(BF16)
 
     def back(self, stage):
-        group, split = self.groups[stage]
-        self.flight = []
-        if not split:
-            return
-        sem = self.bufs[stage][0] + group.size - 1
+        group, _ = self.groups[stage]
+        sem = self.bufs[stage][0] + 1
         rows = self.part(stage, group.index)
         for step in range(1, group.size):
-            copy = self.copy(sem + step - 1, self.total.at[rows, :], self.total.at[rows, :], group.member(group.after(step)))
-            copy.start()
-            came = self.part(stage, lax.rem(group.index + group.size - step, group.size))
-            into = self.copy(sem + step - 1, self.total.at[came, :], self.total.at[came, :], group.member(group.after(step)))
-            self.flight.append((copy, into))
-
-    def arrived(self):
-        for out, into in self.flight:
-            out.wait_send()
-            into.wait_recv()
+            self.copy(sem, self.total.at[rows, :], self.total.at[rows, :], group.member(group.after(step))).start()
+        others = (group.size - 1) * self.rows[stage + 1]
+        self.started(sem, self.total.at[pl.ds(pl.multiple_of(self.base[stage], 16), others), :])
 
     def steps(self):
         last = len(self.groups) - 1
@@ -493,11 +481,14 @@
             self.go(stage)
             yield
             self.add(stage)
-        for stage in range(last, -1, -1):
-            if self.groups[stage][1]:
-                self.back(stage)
-                yield
-                self.arrived()
+        ways = [stage for stage in range(last, -1, -1) if self.groups[stage][1]]
+        for stage in ways:
+            self.back(stage)
+            yield
+            if stage == ways[-1]:
+                for sent in self.owed:
+                    sent.wait_send()
+            self.flight.wait_recv()
 
 
 def groups_of(where, sections, dps):
@@ -593,11 +584,11 @@
                 rows //= group.size
                 shapes.append(pltpu.VMEM((group.size - 1, rows, LANES), BF16))
                 mine.append((sems, len(shapes) - 1))
-                sems += 2 * (group.size - 1)
+                sems += 2
             else:
                 shapes.append(pltpu.VMEM((group.size, rows, LANES), BF16))
                 mine.append((sems, len(shapes) - 1))
-                sems += group.size - 1
+                sems += 1
         where.append(mine)
     return shapes, sems, where
 

time: 50.7 us -> 49.6 us (0.978)
  Pallas kernels: 49.7 us -> 48.6 us
    pallas_call x1, Pallas kernels: 47.1 us -> 46.1 us  [per_device(): pl.pallas_call(partial(body, layers, sections, dps, tuple(sc)), out_shape...]
where the time goes in v3:
time: 49.6 us; the launch traced here: 49.4 us
  Pallas kernels  48.6 us (98%)
  between operations  0.82 us (2%)
    pallas_call x1, Pallas kernels, per_device(): pl.pallas_call(partial(body, layers, sections, dps, tuple(sc)), out_shape...  46.1 us
    pallas_call x1, Pallas kernels, per_device(): pl.pallas_call(partial(finish_body, layers), out_shape=shapes, in_specs=[...  2.56 us

profile of v3, /device:TPU:0, one launch (start us, length us, event | category | flops | bytes accessed | tf_op | source)
XLA Modules:
  0.0 49.4 jit_solution(7349910698468937543)
XLA Ops:
  0.6 46.1 %blocks.1 = (bf16[1,1,196,256]{3,2,1,0:T(8,128)(2,1)S(1)}, bf16[1,1,196,256]{3,2,1,0:T(8,128)(2,1)S(1)}, bf16[10400,128]{1,0:T(8,128)(2,1)S(1)}) custom-call(bf16[1,1,196,256]{3,2,1,0:T(8,128)(2,1)} %refs_0_.1, s32[1,1,2,8,4,49]{5,4,3,2,1,0:T(4,128)} %bitcast.5, bf16[9,2,256]{2,1,0:T(2,128)(2,1)} %bitcast.7, bf16[2,256]{1,0:T(2,128)(2,1)} %refs_3_.1, ...), custom_call_target="tpu_custom_call" | custom-call | tf_op jit(solution)/shard_map/blocks/pallas_call | solution.py:773
  46.7 2.6 %widen.1 = (bf16[1,1,196,256]{3,2,1,0:T(8,128)(2,1)}, bf16[1,1,196,256]{3,2,1,0:T(8,128)(2,1)}, f32[9,2,256]{2,1,0:T(2,128)}, f32[2,256]{1,0:T(2,128)}, f32[2,25...) custom-call(bf16[10400,128]{1,0:T(8,128)(2,1)S(1)} %get-tuple-elemen, ...), custom_call_target="tpu_custom_call" | custom-call | tf_op jit(solution)/shard_map/widen/pallas_call | solution.py:793

commit v4 on v3

--- a/solution.py
+++ b/solution.py
@@ -155,22 +155,26 @@
     eqT = k.eqT[...]
     c = HD**-0.5 * LOG2E
     zkeys = jnp.zeros((FULL - ROWS, FULL), BF16)
-    outs = []
+    outs, scores = [], []
     for half in range(2):
         lanes = slice(half * 128, half * 128 + 128)
         heads = pl.ds(l * HEADS + half * 4, 4)
         rhs = jnp.concatenate([qT[lanes], eqT], 0)
         lhs = jnp.concatenate([head_keys(key[:, lanes]), k.blocked[heads].reshape(4 * ROWS, 128)], 1)
-        s = nn(lhs, rhs).reshape(4, ROWS, FULL)
+        scores.append(nn(lhs, rhs).reshape(4, ROWS, FULL))
+    for half in range(2):
+        heads = pl.ds(l * HEADS + half * 4, 4)
+        s = scores[half]
         m = jnp.max(s, axis=1, keepdims=True)
         e = jnp.exp2((s - m) * c)
-        p = e * (1.0 / jnp.sum(e, axis=1, keepdims=True))
-        k.p[heads] = p
-        pb = p.astype(BF16)
-        k.pb[heads, :ROWS] = pb
+        r = 1.0 / jnp.sum(e, axis=1, keepdims=True)
+        eb = e.astype(BF16)
         for hh in range(4):
             h = half * 4 + hh
-            outs.append(nn(vT[h * HD : (h + 1) * HD], jnp.concatenate([pb[hh], zkeys], 0)))
+            outs.append(nn(vT[h * HD : (h + 1) * HD], jnp.concatenate([eb[hh], zkeys], 0)) * r[hh])
+        p = e * r
+        k.p[heads] = p
+        k.pb[heads, :ROWS] = p.astype(BF16)
     ctx = (jnp.concatenate(outs, 0).T[:ROWS] + k.tmp2[...]).astype(BF16)
     k.ctx[l] = ctx
     k.need(l, "proj")
@@ -247,33 +251,32 @@
     conv_from(k.sd, k.lepef.at[l], 5, True, None, k.tmp2)
 
 
-def attn_bwd_heads(l, k, half):
+def attn_bwd_heads(l, k):
     scale = HD**-0.5
-    lanes = slice(half * 128, half * 128 + 128)
-    heads = pl.ds(l * HEADS + half * 4, 4)
-    dcT = k.dcT[lanes]
-    qT, kT = k.qT[l, lanes], k.kT[l, lanes]
-    dp = nn(head_keys(k.val[l, :, lanes]), dcT).reshape(4, ROWS, FULL)
-    p = k.p[heads]
-    pb = k.pb[heads]
-    pd = p * dp
-    ds = (pd - p * jnp.sum(pd, axis=1, keepdims=True)).astype(BF16)
     zkeys = jnp.zeros((FULL - ROWS, FULL), BF16)
+    grads = []
+    for half in range(2):
+        lanes = slice(half * 128, half * 128 + 128)
+        grads.append(nn(head_keys(k.val[l, :, lanes]), k.dcT[lanes]).reshape(4, ROWS, FULL))
     dq, dk, dv = [], [], []
-    for hh in range(4):
-        rows = slice(hh * HD, (hh + 1) * HD)
-        dsb = jnp.concatenate([ds[hh], zkeys], 0)
-        dv.append(nt(dcT[rows], pb[hh]))
-        dq.append(nn(kT[rows], dsb))
-        dk.append(nt(qT[rows], dsb))
+    for half in range(2):
+        p = k.p[pl.ds(l * HEADS + half * 4, 4)]
+        pd = p * grads[half]
+        ds = (pd - p * jnp.sum(pd, axis=1, keepdims=True)).astype(BF16)
+        for hh in range(4):
+            h = half * 4 + hh
+            rows = slice(h * HD, (h + 1) * HD)
+            dsb = jnp.concatenate([ds[hh], zkeys], 0)
+            dv.append(nt(k.dcT[rows], k.pb[l * HEADS + h]))
+            dq.append(nn(k.kT[l, rows], dsb))
+            dk.append(nt(k.qT[l, rows], dsb))
     dq, dk, dv = (jnp.concatenate(part, 0).T[:ROWS] for part in (dq, dk, dv))
     dq = (dq * scale).astype(BF16)
     dk = (dk * scale).astype(BF16)
-    dv = jnp.where(keep_rows(), dv + k.tmp2[:, lanes], 0.0).astype(BF16)
-    k.dpacked[:, lanes] = dq
-    k.dpacked[:, slice(D + half * 128, D + half * 128 + 128)] = dk
-    k.dpacked[:, slice(2 * D + half * 128, 2 * D + half * 128 + 128)] = dv
-    k.store("qkv%d" % half, l, tn(k.a_normed[l], jnp.concatenate([dq, dk, dv], 1)))
+    dv = jnp.where(keep_rows(), dv + k.tmp2[...], 0.0).astype(BF16)
+    dpacked = jnp.concatenate([dq, dk, dv], 1)
+    k.dpacked[...] = dpacked
+    k.store("qkv", l, tn(k.a_normed[l], dpacked))
 
 
 def attn_bwd_end(l, k):
@@ -518,7 +521,7 @@
 PIECES = (
     (1536, "cpq"),
     (1536, "cpq"),
-    (2048, "cpq"),
+    (2048, "czpW"),
     (1536, "cpq"),
     (1536, "cpq"),
     (512, "cpq"),
@@ -526,17 +529,17 @@
     (160, "cPQ"),
 )
 ORDER = (
-    "wait", "a1", 0, "b1", 1, "s1", 0, "c1", 1, "h1", "k1", 2, "e1", "i1", "a0", 2, 0, 3, "b0", 4, "s0",
-    3, 5, "c0", 1, 4, 5, "h0", 0, "k0", 2, 6, "e0", 1, "i0", "grad", 3, 6, "l1", "p1", "l0", "p0",
-    "last", "out", 0, 4, 5, 2, 7, 7, 1, 3, 6, 4, 2, 5, 0, 7, 3, 0, 6, 1, 4, 5, 1, 7, 2, 7, 6, 2, 3, 3, 4,
-    5, 4, 5, 6, 6,
+    "wait", "a1", 0, "b1", 1, "s1", 0, "c1", 1, "h1", "k1", 2, "e1", "i1", "a0", 2, 3, "b0", 0, 3, 4,
+    "s0", 5, "c0", "h0", 1, 4, 5, "k0", 2, 6, "e0", "i0", "grad", 0, 3, 6, 1, "l1", "p1", "l0", "p0",
+    "last", "out", 4, 7, 5, 7, 2, 3, 0, 1, 6, 4, 5, 7, 2, 3, 0, 6, 0, 4, 1, 1, 2, 5, 7, 7, 6, 3, 3, 4, 5,
+    4, 5, 2, 6, 2, 6,
 )
 
 
 def row_map(layers):
     at, n = {}, 0
     for l in reversed(range(layers)):
-        for name, rows in (("fc2", 6 * D), ("fc1", 6 * D), ("proj", 2 * D), ("qkv0", 3 * D), ("qkv1", 3 * D)):
+        for name, rows in (("fc2", 6 * D), ("fc1", 6 * D), ("proj", 2 * D), ("qkv", 6 * D)):
             at[name, l] = n
             n += rows
     at["last"] = n
@@ -686,8 +689,8 @@
             ("s", attn_bwd_start),
             ("l", attn_bwd_lepe),
             ("c", attn_bwd_conv),
-            ("h", partial(attn_bwd_heads, half=0)),
-            ("k", partial(attn_bwd_heads, half=1)),
+            ("h", attn_bwd_heads),
+            ("k", lambda l, k: None),
             ("e", attn_bwd_end),
             ("i", attn_bwd_input),
             ("p", attn_bwd_pos),
@@ -732,7 +735,7 @@
         wide("fc2", l, [(at["fc2", l] + c * 3 * D, 3 * D, 0, c * LANES) for c in range(2)])
         wide("fc1", l, [(at["fc1", l] + c * D, D, 0, c * LANES) for c in range(6)])
         wide("proj", l, [(at["proj", l] + c * D, D, 0, c * LANES) for c in range(2)])
-        wide("qkv", l, [(at["qkv%d" % h, l] + c * D, D, 0, c * D + h * LANES) for c in range(3) for h in range(2)])
+        wide("qkv", l, [(at["qkv", l] + c * D, D, 0, c * LANES) for c in range(6)])
 
     def rows_from(n, count):
         return [total[pl.ds(n + c * count, count), :].astype(F32) for c in range(2)]

time: 49.6 us -> 47.5 us (0.958)
  Pallas kernels: 48.6 us -> 46.5 us
    pallas_call x1, Pallas kernels: 46.1 us -> 43.9 us  [per_device(): pl.pallas_call(partial(body, layers, sections, dps, tuple(sc)), out_shape...]
where the time goes in v4:
time: 47.5 us; the launch traced here: 47.3 us
  Pallas kernels  46.5 us (98%)
  between operations  0.82 us (2%)
    pallas_call x1, Pallas kernels, per_device(): pl.pallas_call(partial(body, layers, sections, dps, tuple(sc)), out_shape...  43.9 us
    pallas_call x1, Pallas kernels, per_device(): pl.pallas_call(partial(finish_body, layers), out_shape=shapes, in_specs=[...  2.56 us

profile of v4, /device:TPU:0, one launch (start us, length us, event | category | flops | bytes accessed | tf_op | source)
XLA Modules:
  0.0 47.3 jit_solution(7712989036447100540)
XLA Ops:
  0.6 43.9 %blocks.1 = (bf16[1,1,196,256]{3,2,1,0:T(8,128)(2,1)S(1)}, bf16[1,1,196,256]{3,2,1,0:T(8,128)(2,1)S(1)}, bf16[10400,128]{1,0:T(8,128)(2,1)S(1)}) custom-call(bf16[1,1,196,256]{3,2,1,0:T(8,128)(2,1)} %refs_0_.1, s32[1,1,2,8,4,49]{5,4,3,2,1,0:T(4,128)} %bitcast.5, bf16[9,2,256]{2,1,0:T(2,128)(2,1)} %bitcast.7, bf16[2,256]{1,0:T(2,128)(2,1)} %refs_3_.1, ...), custom_call_target="tpu_custom_call" | custom-call | tf_op jit(solution)/shard_map/blocks/pallas_call | solution.py:776
  44.6 2.6 %widen.1 = (bf16[1,1,196,256]{3,2,1,0:T(8,128)(2,1)}, bf16[1,1,196,256]{3,2,1,0:T(8,128)(2,1)}, f32[9,2,256]{2,1,0:T(2,128)}, f32[2,256]{1,0:T(2,128)}, f32[2,25...) custom-call(bf16[10400,128]{1,0:T(8,128)(2,1)S(1)} %get-tuple-elemen, ...), custom_call_target="tpu_custom_call" | custom-call | tf_op jit(solution)/shard_map/widen/pallas_call | solution.py:796

commit v5 on v4

--- a/solution.py
+++ b/solution.py
@@ -400,7 +400,11 @@
         return tuple(at)
 
     def after(self, step):
-        return lax.rem(self.index + step, self.size)
+        if self.size != 4:
+            return lax.rem(self.index + step, self.size)
+        first = (3 - self.index, self.index + 1 - 2 * lax.rem(self.index, 2), self.index + 2 - 4 * (self.index // 2))
+        second = (self.index + 1 - 2 * lax.rem(self.index, 2), self.index + 2 - 4 * (self.index // 2), 3 - self.index)
+        return (first if self.axis == 0 else second)[step - 1]
 
 
 class Exchange:

time: 47.5 us -> 47.5 us (level)
  no operation moved by 1% of the time
where the time goes in v5:
time: 47.5 us; the launch traced here: 47.3 us
  Pallas kernels  46.5 us (98%)
  between operations  0.82 us (2%)
    pallas_call x1, Pallas kernels, per_device(): pl.pallas_call(partial(body, layers, sections, dps, tuple(sc)), out_shape...  43.9 us
    pallas_call x1, Pallas kernels, per_device(): pl.pallas_call(partial(finish_body, layers), out_shape=shapes, in_specs=[...  2.56 us

profile of v5, /device:TPU:0, one launch (start us, length us, event | category | flops | bytes accessed | tf_op | source)
XLA Modules:
  0.0 47.3 jit_solution(3470332284050510905)
XLA Ops:
  0.6 43.9 %blocks.1 = (bf16[1,1,196,256]{3,2,1,0:T(8,128)(2,1)S(1)}, bf16[1,1,196,256]{3,2,1,0:T(8,128)(2,1)S(1)}, bf16[10400,128]{1,0:T(8,128)(2,1)S(1)}) custom-call(bf16[1,1,196,256]{3,2,1,0:T(8,128)(2,1)} %refs_0_.1, s32[1,1,2,8,4,49]{5,4,3,2,1,0:T(4,128)} %bitcast.5, bf16[9,2,256]{2,1,0:T(2,128)(2,1)} %bitcast.7, bf16[2,256]{1,0:T(2,128)(2,1)} %refs_3_.1, ...), custom_call_target="tpu_custom_call" | custom-call | tf_op jit(solution)/shard_map/blocks/pallas_call | solution.py:780
  44.6 2.6 %widen.1 = (bf16[1,1,196,256]{3,2,1,0:T(8,128)(2,1)}, bf16[1,1,196,256]{3,2,1,0:T(8,128)(2,1)}, f32[9,2,256]{2,1,0:T(2,128)}, f32[2,256]{1,0:T(2,128)}, f32[2,25...) custom-call(bf16[10400,128]{1,0:T(8,128)(2,1)S(1)} %get-tuple-elemen, ...), custom_call_target="tpu_custom_call" | custom-call | tf_op jit(solution)/shard_map/widen/pallas_call | solution.py:800
